TPU v7x, 256 devices: a whole 4x4x8 slice. The times are simulated.
256 devices in a mesh: coarse: 32 (over z, x), fine: 8 (over y, core).
Axes of the slice: x: 4, y: 4, z: 8, core: 2. Of those that a mesh axis runs over, the one named last changes fastest.
Arguments:
- node_feats: bfloat16 [524288, 256], P(('coarse', 'fine')), may hold values from -6 to 6
- grad_out: bfloat16 [524288, 256], P(('coarse', 'fine')), may hold values from -6 to 6
- cluster_ids: int32 [524288], P(('coarse', 'fine')), may hold values from 0 to 65535, as said below
- halo_lists: int32 [8192], P('coarse'), may hold values from 0 to 2047, as said below
- edge_sources: int32 [262144], P('coarse'), may hold values from 0 to 2303, as said below
- w_edge_in: bfloat16 [512, 256], replicated, may hold values from -0.25 to 0.25
- b_edge_in: bfloat16 [256], replicated, may hold values from -4 to 4
- w_edge_out: bfloat16 [256, 256], replicated, may hold values from -0.375 to 0.375
- w_unpool: bfloat16 [256, 256], replicated, may hold values from -0.375 to 0.375
Outputs:
- grad_feats: bfloat16 [524288, 256], P(('coarse', 'fine'))
- grad_w_in: float32 [512, 256], replicated
- grad_b_in: float32 [256], replicated
- grad_w_out: float32 [256, 256], replicated
- grad_unpool: float32 [256, 256], replicated
Inputs may be any that keep to these rules, and one draw needn't show every extreme that they name: `cluster_ids`: the fine nodes on the devices of coarse index g lie in cells g*2048 to (g+1)*2048 - 1. `halo_lists`: each owner's block of 256 entries holds distinct indices. `edge_sources`: each owner's block of 8192 entries takes every value of its range at least once.
All inputs are finite; a program needn't handle non-finite values.
Results may differ from a plain program's by a relative error of at most 0.0065.
Values may be sent and summed in bfloat16 or wider, within the bound.
A program may use at most 128 MiB of HBM per device.

v0:
```python
import jax
import jax.numpy as jnp
from jax import lax
from jax.sharding import PartitionSpec as P

K = 4


def with_halo(cells, sides, width):
    for axis, dim in sides:
        count = lax.axis_size(axis)
        head = lax.slice_in_dim(cells, 0, width, axis=dim)
        tail = lax.slice_in_dim(cells, cells.shape[dim] - width, cells.shape[dim], axis=dim)
        cells = jnp.concatenate(
            [
                lax.ppermute(tail, axis, [(i, (i + 1) % count) for i in range(count)]),
                cells,
                lax.ppermute(head, axis, [((i + 1) % count, i) for i in range(count)]),
            ],
            axis=dim,
        )
    return cells


def edge_work(
    dst_bf, dst_full, extended, sources, grad_sum_bf, w_edge_in, b_edge_in, w_edge_out, w_unpool
):
    row_count = dst_bf.shape[0]
    feature_width = dst_bf.shape[1]
    fan_count = sources.shape[0] // row_count
    dst_rep = jnp.repeat(dst_bf, fan_count, axis=0)
    src_feats = jnp.take(extended, sources, axis=0)
    joined = jnp.concatenate([dst_rep, src_feats], axis=1)
    pre_act = jnp.dot(joined, w_edge_in, preferred_element_type=jnp.float32) + b_edge_in.astype(
        jnp.float32
    )
    sigmoid_act = jax.nn.sigmoid(pre_act)
    hidden = (pre_act * sigmoid_act).astype(jnp.bfloat16)
    messages = jnp.dot(hidden, w_edge_out, preferred_element_type=jnp.float32)
    aggregate = messages.reshape(row_count, fan_count, feature_width).sum(axis=1)
    new_coarse = (dst_full + aggregate).astype(jnp.bfloat16)
    grad_new = jnp.dot(grad_sum_bf, w_unpool.T, preferred_element_type=jnp.float32).astype(
        jnp.bfloat16
    )
    grad_up = jnp.dot(new_coarse.T, grad_sum_bf, preferred_element_type=jnp.float32)
    grad_msg = jnp.repeat(grad_new, fan_count, axis=0)
    grad_w2 = jnp.dot(hidden.T, grad_msg, preferred_element_type=jnp.float32)
    grad_hidden = jnp.dot(grad_msg, w_edge_out.T, preferred_element_type=jnp.float32)
    grad_act = (grad_hidden * sigmoid_act * (1.0 + pre_act * (1.0 - sigmoid_act))).astype(
        jnp.bfloat16
    )
    grad_w1 = jnp.dot(joined.T, grad_act, preferred_element_type=jnp.float32)
    grad_b1 = jnp.sum(grad_act.astype(jnp.float32), axis=0)
    grad_joined = jnp.dot(grad_act, w_edge_in.T, preferred_element_type=jnp.float32)
    grad_dst = grad_new.astype(jnp.float32) + grad_joined[:, :feature_width].reshape(
        row_count, fan_count, feature_width
    ).sum(axis=1)
    grad_src = jax.ops.segment_sum(
        grad_joined[:, feature_width:], sources, num_segments=extended.shape[0]
    )
    return (grad_dst, grad_src, grad_up, grad_w2, grad_w1, grad_b1)


def extend_rows(pooled_bf, right_ids, left_ids):
    half_rows = right_ids.shape[0]
    outgoing = jnp.concatenate(
        [jnp.take(pooled_bf, left_ids, axis=0), jnp.take(pooled_bf, right_ids, axis=0)], axis=0
    )
    arrived = with_halo(outgoing, (("coarse", 0),), half_rows)
    return jnp.concatenate([pooled_bf, arrived[:half_rows], arrived[3 * half_rows :]], axis=0)


def return_rows(grad_src, right_ids, left_ids, cell_count):
    half_rows = right_ids.shape[0]
    arrived = with_halo(
        grad_src[cell_count:].astype(jnp.bfloat16), (("coarse", 0),), half_rows
    ).astype(jnp.float32)
    for_left = arrived[:half_rows]
    for_right = arrived[3 * half_rows :]
    return jax.ops.segment_sum(for_left, left_ids, num_segments=cell_count) + jax.ops.segment_sum(
        for_right, right_ids, num_segments=cell_count
    )


def local(
    node_feats,
    grad_out,
    cluster_ids,
    halo_lists,
    edge_sources,
    w_edge_in,
    b_edge_in,
    w_edge_out,
    w_unpool,
):
    fan_count = K
    cell_count = edge_sources.shape[0] // fan_count
    half_rows = halo_lists.shape[0] // 2
    owner_index = lax.axis_index("coarse")
    local_ids = cluster_ids - owner_index * cell_count
    part_feats = jax.ops.segment_sum(
        node_feats.astype(jnp.float32), local_ids, num_segments=cell_count
    )
    part_grads = jax.ops.segment_sum(
        grad_out.astype(jnp.float32), local_ids, num_segments=cell_count
    )
    right_ids = halo_lists[:half_rows]
    left_ids = halo_lists[half_rows:]
    pooled, grad_sum = lax.psum((part_feats, part_grads), "fine")
    pooled_bf = pooled.astype(jnp.bfloat16)
    extended = extend_rows(pooled_bf, right_ids, left_ids)
    grad_dst, grad_src, grad_up, grad_w2, grad_w1, grad_b1 = edge_work(
        pooled_bf,
        pooled,
        extended,
        edge_sources,
        grad_sum.astype(jnp.bfloat16),
        w_edge_in,
        b_edge_in,
        w_edge_out,
        w_unpool,
    )
    grad_pool = (
        grad_dst + grad_src[:cell_count] + return_rows(grad_src, right_ids, left_ids, cell_count)
    )
    grad_w1, grad_b1, grad_w2, grad_up = lax.psum((grad_w1, grad_b1, grad_w2, grad_up), "coarse")
    grad_feats = (grad_out.astype(jnp.float32) + jnp.take(grad_pool, local_ids, axis=0)).astype(
        jnp.bfloat16
    )
    total_cells = cell_count * lax.axis_size("coarse")
    total_edges = total_cells * fan_count
    edge_scale = float(total_edges) ** (-0.5)
    cell_scale = float(total_cells) ** (-0.5)
    return (
        grad_feats,
        grad_w1 * edge_scale,
        grad_b1 * edge_scale,
        grad_w2 * edge_scale,
        grad_up * cell_scale,
    )


def solution(mesh):
    return jax.shard_map(
        local,
        mesh=mesh,
        in_specs=(
            P(("coarse", "fine"), None),
            P(("coarse", "fine"), None),
            P(("coarse", "fine")),
            P("coarse"),
            P("coarse"),
            P(),
            P(),
            P(),
            P(),
        ),
        out_specs=(P(("coarse", "fine"), None), P(), P(), P(), P()),
        check_vma=False,
    )
```

profile of v0, /device:TPU:8, one launch (start us, length us, event | category | flops | bytes accessed | tf_op | source)
XLA Modules:
  0.0 454.5 jit_solution(3173764791918787573)
XLA Ops:
  8.1 12.4 %scatter_custom_fusion.1 = f32[2048,256]{1,0:T(8,128)} fusion(s32[2048]{0:T(1024)S(1)} %get-tuple-element.10, bf16[2048,256]{1,0:T(8,128)(2,1)} %param.11, f32[]{:T(128)} %constant.35.clone.1), kind=kCustom, calls=%fused_computation.27 | custom fusion | flops 1048576 | bytes 3145732 | tf_op jit(solution)/shard_map/scatter-add | solution.py:101
  21.0 12.1 %scatter_custom_fusion = f32[2048,256]{1,0:T(8,128)S(1)} fusion(s32[2048]{0:T(1024)S(1)} %get-tuple-element.10, bf16[2048,256]{1,0:T(8,128)(2,1)S(1)} %copy-done.11, f32[]{:T(128)} %constant.35.clone.1), kind=kCustom, calls=%fused_computation.21 | custom fusion | flops 1048576 | bytes 3145732 | tf_op jit(solution)/shard_map/scatter-add | solution.py:104
  33.2 56.8 %all-reduce.8 = bf16[2048,256]{1,0:T(8,128)(2,1)S(1)} all-reduce(f32[2048,256]{1,0:T(8,128)S(1)} %scatter_custom_fusion), channel_id=1, replica_groups=mesh['coarse'=32,'fine'=8] {'fine'}, use_global_device_ids=true, to_apply=%region_1.0 | all-reduce | flops 524288 | bytes 3145728 | tf_op jit(solution)/shard_map/psum | solution.py:109
  91.8 2.9 broadcast_in_dim.58
  94.7 6.9 %reshape.38 = bf16[8192,256]{1,0:T(8,128)(2,1)} reshape(bf16[2048,4,256]{2,1,0:T(4,128)(2,1)} %broadcast_in_dim.58) | data formatting | bytes 8388608 | tf_op jit(solution)/shard_map/reshape | solution.py:46
  101.8 1.7 convert_element_type.46
  106.9 6.8 %collective-permute-start.1 = (bf16[128,256]{1,0:T(8,128)(2,1)S(1)}, bf16[128,256]{1,0:T(8,128)(2,1)S(1)}, u32[]{:S(2)}, u32[]{:S(2)}) collective-permute-start(bf16[128,256]{1,0:T(8,128)(2,1)S(1)} %broadcast_select_fusion.1), channel_id=1, source_target_pairs={{8,0},{16,8},{24,16},{32,24},{40,32},{48,40},{56,48},{64,56},{72,6... | collective-permute-start | bytes 196616 | tf_op jit(solution)/shard_map/ppermute | solution.py:18
  113.7 2.9 broadcast_in_dim.59
  116.6 6.9 %reshape.39 = bf16[8192,256]{1,0:T(8,128)(2,1)} reshape(bf16[2048,4,256]{2,1,0:T(4,128)(2,1)} %broadcast_in_dim.59) | data formatting | bytes 8388608 | tf_op jit(solution)/shard_map/reshape | solution.py:31
  123.7 32.9 %gather_fusion = bf16[8192,256]{1,0:T(8,128)(2,1)} fusion(bf16[2304,256]{1,0:T(8,128)(2,1)S(1)} %pad_maximum_fusion.3, s32[8192]{0:T(1024)S(1)} %fusion.21), kind=kCustom, calls=%fused_computation.2 | custom fusion | bytes 8421376 | tf_op jit(solution)/shard_map/jit(_take)/gather | solution.py:32
  156.6 6.1 %broadcast_select_fusion = bf16[8192,256]{1,0:T(8,128)(2,1)S(1)} fusion(bf16[8192,256]{1,0:T(8,128)(2,1)} %gather_fusion, pred[8192]{0:T(1024)(128)(4,1)S(1)} %compare_and_fusion), kind=kLoop, calls=%fused_computation.19 | loop fusion | flops 2097152 | bytes 8396800 | tf_op jit(solution)/shard_map/jit(_take)/select_n | solution.py:32
  162.7 2.4 multiply_convert_fusion
  165.1 2.0 fusion.27
  167.1 4.5 fusion.28
  171.6 3.8 convert_reduce_fusion
  175.4 3.2 fusion.4
  178.6 8.1 %fusion.26 = f32[8192,512]{1,0:T(8,128)} fusion(bf16[8192,256]{1,0:T(8,128)(2,1)S(1)} %get-tuple-element.26, bf16[512,256]{1,0:T(8,128)(2,1)S(1)} %copy-done), kind=kOutput, calls=%fused_computation.69 | convolution fusion | flops 2147483648 | bytes 21233664 | tf_op jit(solution)/shard_map/dot_general | solution.py:54
  186.7 45.7 %scatter_custom_fusion.2 = f32[2304,256]{1,0:T(8,128)S(1)} fusion(s32[8192]{0:T(1024)S(1)} %copy-done.15, f32[8192,512]{1,0:T(8,128)} %fusion.26, f32[]{:T(128)} %constant.35.clone.1), kind=kCustom, calls=%fused_computation.12 | custom fusion | flops 2097152 | bytes 10748416 | tf_op jit(solution)/shard_map/scatter-add | solution.py:58
  232.4 8.0 %slice.51 = f32[8192,256]{1,0:T(8,128)} slice(f32[8192,512]{1,0:T(8,128)} %fusion.26), slice={[0:8192], [0:256]} | slice | bytes 16777216 | tf_op jit(solution)/shard_map/slice | solution.py:55
  240.5 10.0 %reshape.41 = f32[2048,4,256]{2,1,0:T(4,128)} reshape(f32[8192,256]{1,0:T(8,128)} %fusion.28) | data formatting | bytes 16777216 | tf_op jit(solution)/shard_map/reshape | solution.py:40
  250.4 13.8 %reduce_sum.29 = f32[2048,256]{1,0:T(8,128)} reduce(f32[2048,4,256]{2,1,0:T(4,128)} %reshape.41, f32[]{:T(128)} %constant.35.clone.1), dimensions={1}, to_apply=%region_11.13 | reduce | flops 1572864 | bytes 10485764 | tf_op jit(solution)/shard_map/reduce_sum | solution.py:40
  264.2 9.8 %reshape.40 = f32[2048,4,256]{2,1,0:T(4,128)} reshape(f32[8192,256]{1,0:T(8,128)} %slice.51) | data formatting | bytes 16777216 | tf_op jit(solution)/shard_map/reshape | solution.py:55
  274.0 13.8 %reduce_sum.27 = f32[2048,256]{1,0:T(8,128)} reduce(f32[2048,4,256]{2,1,0:T(4,128)} %reshape.40, f32[]{:T(128)} %constant.35.clone.1), dimensions={1}, to_apply=%region_4.0 | reduce | flops 1572864 | bytes 10485764 | tf_op jit(solution)/shard_map/reduce_sum | solution.py:57
  290.1 2.1 slice_add_fusion
  295.5 5.3 %collective-permute-start.3 = (bf16[128,256]{1,0:T(8,128)(2,1)S(1)}, bf16[128,256]{1,0:T(8,128)(2,1)S(1)}, u32[]{:S(2)}, u32[]{:S(2)}) collective-permute-start(bf16[128,256]{1,0:T(8,128)(2,1)S(1)} %get-tuple-element.16), channel_id=1, source_target_pairs={{8,0},{16,8},{24,16},{32,24},{40,32},{48,40},{56,48},{64,56},{72,6... | collective-permute-start | bytes 196616 | tf_op jit(solution)/shard_map/ppermute | solution.py:18
  300.8 69.6 %psum.45 = f32[256]{0:T(256)S(1)} all-reduce(f32[256]{0:T(256)S(1)} %get-tuple-element.25), channel_id=1, replica_groups=mesh['coarse'=32,'fine'=8] {'coarse'}, use_global_device_ids=true, to_apply=%region_9.11 | all-reduce | flops 256 | bytes 2048 | tf_op jit(solution)/shard_map/psum | solution.py:126
  372.0 2.7 scatter_custom_fusion.3
  374.8 8.6 %gather_fusion.1 = f32[2048,256]{1,0:T(8,128)} fusion(f32[2048,256]{1,0:T(8,128)S(1)} %scatter_custom_fusion.3, s32[2048]{0:T(1024)S(1)} %fusion.22), kind=kCustom, calls=%fused_computation.3 | custom fusion | bytes 4202496 | tf_op jit(solution)/shard_map/jit(_take)/gather | solution.py:127
  383.4 2.5 fusion.7
  385.9 57.8 %all-reduce.7.cloned.1.call-done = (f32[512,256]{1,0:T(8,128)}, f32[256,256]{1,0:T(8,128)}, f32[256,256]{1,0:T(8,128)}) async-done(((f32[512,256]{1,0:T(8,128)}, f32[256,256]{1,0:T(8,128)}, f32[256,256]{1,0:T(8,128)}), (f32[512,256]{1,0:T(8,128)}, f32[256,256]{1,0:T(8,128)}, f32[256,256]{1,0:T(8,128)})) %all-reduce.7.cloned.1.call-update) | async-done | bytes 1048592 | tf_op jit(solution)/shard_map/psum | solution.py:126
  443.7 1.9 broadcast_multiply_fusion
  445.6 1.9 broadcast_multiply_fusion.1
  (73 shorter events, 13.9 us)
Async XLA Ops:
  7.2 155.6 %copy-start = (bf16[512,256]{1,0:T(8,128)(2,1)S(1)}, bf16[512,256]{1,0:T(8,128)(2,1)}, u32[]{:S(2)}) copy-start(bf16[512,256]{1,0:T(8,128)(2,1)} %param.16) | copy-start | bytes 786436
  7.2 13.3 %copy-start.16 = (s32[256]{0:T(256)S(1)}, s32[256]{0:T(256)}, u32[]{:S(2)}) copy-start(s32[256]{0:T(256)} %param.14) | copy-start | bytes 3076
  7.2 13.9 %copy-start.11 = (bf16[2048,256]{1,0:T(8,128)(2,1)S(1)}, bf16[2048,256]{1,0:T(8,128)(2,1)}, u32[]{:S(2)}) copy-start(bf16[2048,256]{1,0:T(8,128)(2,1)} %param.12) | copy-start | bytes 3145732
  7.2 94.6 %all-reduce.5.cloned.1.call-start = ((), (), s32[]{:S(2)}) async-start(), calls=%async_computation | async-start | bytes 4194304 | tf_op jit(solution)/shard_map/psum | solution.py:109
  20.4 69.6 %copy-start.14 = (bf16[256,256]{1,0:T(8,128)(2,1)S(1)}, bf16[256,256]{1,0:T(8,128)(2,1)}, u32[]{:S(2)}) copy-start(bf16[256,256]{1,0:T(8,128)(2,1)} %param.19) | copy-start | bytes 393220
  20.5 423.3 %all-reduce.7.cloned.1.call-start = ((), (), s32[]{:S(2)}) async-start(), calls=%async_computation.1 | async-start | bytes 2097152 | tf_op jit(solution)/shard_map/psum | solution.py:126
  90.0 11.6 %copy-start.5 = (bf16[2048,256]{1,0:T(8,128)(2,1)}, bf16[2048,256]{1,0:T(8,128)(2,1)S(1)}, u32[]{:S(2)}) copy-start(bf16[2048,256]{1,0:T(8,128)(2,1)S(1)} %all-reduce.8) | copy-start | bytes 3145732
  90.5 1.4 copy-start.3
  94.7 6.9 %copy-start.19 = (s32[128]{0:T(128)S(1)}, s32[128]{0:T(128)}, u32[]{:S(2)}) copy-start(s32[128]{0:T(128)} %get-tuple-element.22) | copy-start | bytes 1540
  94.7 7.0 %copy-start.15 = (s32[8192]{0:T(1024)S(1)}, s32[8192]{0:T(1024)}, u32[]{:S(2)}) copy-start(s32[8192]{0:T(1024)} %param.15) | copy-start | bytes 98308
  101.6 3.5 copy-start.18
  101.6 5.2 %copy-start.17 = (pred[128]{0:T(512)(128)(4,1)S(1)}, pred[128]{0:T(512)(128)(4,1)}, u32[]{:S(2)}) copy-start(pred[128]{0:T(512)(128)(4,1)} %get-tuple-element.21) | copy-start | bytes 388
  105.3 18.3 %collective-permute-start = (bf16[128,256]{1,0:T(8,128)(2,1)S(1)}, bf16[128,256]{1,0:T(8,128)(2,1)S(1)}, u32[]{:S(2)}, u32[]{:S(2)}) collective-permute-start(bf16[128,256]{1,0:T(8,128)(2,1)S(1)} %broadcast_select_fusion.2), channel_id=1, source_target_pairs={{0,8},{8,16},{16,24},{24,32},{32,40},{40,48},{48,56},{56,64},{64,7... | collective-permute-start | bytes 196616 | tf_op jit(solution)/shard_map/ppermute | solution.py:16
  106.9 16.7 %collective-permute-start.1 = (bf16[128,256]{1,0:T(8,128)(2,1)S(1)}, bf16[128,256]{1,0:T(8,128)(2,1)S(1)}, u32[]{:S(2)}, u32[]{:S(2)}) collective-permute-start(bf16[128,256]{1,0:T(8,128)(2,1)S(1)} %broadcast_select_fusion.1), channel_id=1, source_target_pairs={{8,0},{16,8},{24,16},{32,24},{40,32},{48,40},{56,48},{64,56},{72,6... | collective-permute-start | bytes 196616 | tf_op jit(solution)/shard_map/ppermute | solution.py:18
  156.6 6.1 %copy-start.10 = (bf16[8192,256]{1,0:T(8,128)(2,1)S(1)}, bf16[8192,256]{1,0:T(8,128)(2,1)}, u32[]{:S(2)}) copy-start(bf16[8192,256]{1,0:T(8,128)(2,1)} %reshape.39) | copy-start | bytes 12582916
  162.7 2.4 copy-start.1
  165.1 2.0 copy-start.13
  232.4 55.3 %copy-start.2 = (f32[2304,256]{1,0:T(8,128)}, f32[2304,256]{1,0:T(8,128)S(1)}, u32[]{:S(2)}) copy-start(f32[2304,256]{1,0:T(8,128)S(1)} %scatter_custom_fusion.2) | copy-start | bytes 7077892
  287.8 1.7 copy-start.4
  287.8 2.3 copy-start.8
  290.1 2.1 copy-start.6
  290.1 2.5 copy-start.7
  290.1 3.2 copy-start.9
  295.4 76.5 %collective-permute-start.2 = (bf16[128,256]{1,0:T(8,128)(2,1)S(1)}, bf16[128,256]{1,0:T(8,128)(2,1)S(1)}, u32[]{:S(2)}, u32[]{:S(2)}) collective-permute-start(bf16[128,256]{1,0:T(8,128)(2,1)S(1)} %get-tuple-element.15), channel_id=1, source_target_pairs={{0,8},{8,16},{16,24},{24,32},{32,40},{40,48},{48,56},{56,64},{64,7... | collective-permute-start | bytes 196616 | tf_op jit(solution)/shard_map/ppermute | solution.py:16
  295.5 76.5 %collective-permute-start.3 = (bf16[128,256]{1,0:T(8,128)(2,1)S(1)}, bf16[128,256]{1,0:T(8,128)(2,1)S(1)}, u32[]{:S(2)}, u32[]{:S(2)}) collective-permute-start(bf16[128,256]{1,0:T(8,128)(2,1)S(1)} %get-tuple-element.16), channel_id=1, source_target_pairs={{8,0},{16,8},{24,16},{32,24},{40,32},{48,40},{56,48},{64,56},{72,6... | collective-permute-start | bytes 196616 | tf_op jit(solution)/shard_map/ppermute | solution.py:18
  374.8 8.6 %copy-start.12 = (bf16[2048,256]{1,0:T(8,128)(2,1)S(1)}, bf16[2048,256]{1,0:T(8,128)(2,1)}, u32[]{:S(2)}) copy-start(bf16[2048,256]{1,0:T(8,128)(2,1)} %param.12) | copy-start | bytes 3145732
Sparse Core Ops, SparseCore 0:
  20.6 75.4 all-reduce.4
  294.7 149.0 all-reduce.6
where the time goes:
time: 462 us; the launch traced here: 454 us
  blocking collectives  126 us (27%)
  other arithmetic  121 us (26%)
  local copies, waits for them, and re-layouts  94.8 us (21%)
  waiting for transfers between devices  57.9 us (13%)
  matrix products  25.6 us (6%)
  between operations  14.6 us (3%)
  starting transfers between devices  13.8 us (3%)
    psum x1, blocking collectives, local(): lax.psum((grad_w1, grad_b1, grad_w2, grad_up), 'coarse')  69.6 us
    psum x1, waiting for transfers between devices, local(): lax.psum((grad_w1, grad_b1, grad_w2, grad_up), 'coarse')  57.8 us
    psum x1, blocking collectives, local(): pooled, grad_sum = lax.psum((part_feats, part_grads), 'fine')  56.8 us
    scatter-add x1, other arithmetic, edge_work(): jax.ops.segment_sum(grad_joined[:, feature_width:], sources, num_segments...  45.7 us
    gather x1, local copies, waits for them, and re-layouts, edge_work(): src_feats = jnp.take(extended, sources, axis=0)  32.9 us
    reduce_sum x1, other arithmetic, edge_work(): messages.reshape(row_count, fan_count, feature_width).sum(axis=1)  13.8 us
    reduce_sum x1, other arithmetic, edge_work(): grad_dst = grad_new.astype(jnp.float32) + grad_joined[:, :feature_width]....  13.8 us
    scatter-add x1, other arithmetic, local(): jax.ops.segment_sum(node_feats.astype(jnp.float32), local_ids, num_segmen...  12.4 us
  transfers between devices with their start and end apart: 6, of which 1 were waited for; matrix products, arithmetic and copies ran while one was open for 11% of the time, Pallas kernels for 0%

commit v1 on v0

v1 whole, which is shorter than its diff:
```python
import functools

import jax
import jax.numpy as jnp
from jax import lax
from jax.experimental import pallas as pl
from jax.experimental.pallas import tpu as pltpu
from jax.sharding import PartitionSpec as P

MESH = pl.DeviceIdType.MESH
F32 = jnp.float32
BF16 = jnp.bfloat16
I32 = jnp.int32
K = 4
NY = 4
L = 128


def dot(a, b, dims=((1,), (0,))):
    return lax.dot_general(a, b, (dims, ((), ())), preferred_element_type=F32)


def onehot(mask):
    return jnp.where(mask, 1.0, 0.0).astype(BF16)


def columns(row):
    return jnp.transpose(jnp.broadcast_to(row, (L, L)))


class Scatter:
    def __init__(self, place, stage, psend, prcv, ysend, yrcv, sems):
        self.p = place
        self.stage, self.psend, self.prcv = stage, psend, prcv
        self.ysend, self.yrcv = ysend, yrcv
        self.ps, self.pr, self.ys, self.yr = sems
        self.cells = psend.shape[1]
        self.half = self.cells // 2

    def pair(self, r):
        return pltpu.make_async_remote_copy(
            src_ref=self.psend.at[r], dst_ref=self.prcv.at[r],
            send_sem=self.ps.at[r], recv_sem=self.pr.at[r],
            device_id={"fine": self.p["partner"]}, device_id_type=MESH)

    def ring(self, i):
        to = self.p["up"] if i in (0, 2, 4) else self.p["down"]
        return pltpu.make_async_remote_copy(
            src_ref=self.ysend.at[i], dst_ref=self.yrcv.at[i],
            send_sem=self.ys.at[i], recv_sem=self.yr.at[i],
            device_id={"fine": to}, device_id_type=MESH)

    def emit_pair(self, r):
        at = pl.multiple_of((1 - self.p["core"]) * self.cells, self.cells)
        self.psend[r] = self.stage[r, pl.ds(at, self.cells), :].astype(BF16)
        self.pair(r).start()

    def half_sum(self, r, h):
        at = pl.multiple_of(self.p["core"] * self.cells + h * self.half, self.half)
        mine = self.stage[r, pl.ds(at, self.half), :]
        return mine + self.prcv[r, h * self.half:(h + 1) * self.half, :].astype(F32)

    def send(self, i, value):
        self.ysend[i] = value.astype(BF16)
        self.ring(i).start()

    def far(self):
        self.pair(2).wait_recv()
        self.send(0, self.half_sum(2, 0))
        self.send(1, self.half_sum(2, 1))

    def near_up(self):
        self.pair(1).wait_recv()
        self.send(2, self.half_sum(1, 1))

    def near_down(self):
        self.pair(3).wait_recv()
        self.send(3, self.half_sum(3, 0))

    def relay(self):
        self.ring(0).wait_recv()
        self.send(4, self.half_sum(1, 0) + self.yrcv[0].astype(F32))
        self.ring(1).wait_recv()
        self.send(5, self.half_sum(3, 1) + self.yrcv[1].astype(F32))

    def finish(self):
        self.pair(0).wait_recv()
        for i in (2, 3, 4, 5):
            self.ring(i).wait_recv()
        low = self.half_sum(0, 0) + self.yrcv[4].astype(F32) + self.yrcv[3].astype(F32)
        high = self.half_sum(0, 1) + self.yrcv[2].astype(F32) + self.yrcv[5].astype(F32)
        return low, high

    def drain(self):
        for r in range(NY):
            self.pair(r).wait_send()
        for i in range(6):
            self.ring(i).wait_send()


class Gather:
    def __init__(self, place, table, cells, sems):
        self.p, self.table, self.cells = place, table, cells
        self.half = cells // 2
        self.ss, self.rs = sems

    def copy(self, i, to, y, core, h0, rows):
        at = pl.multiple_of((y * 2 + core) * self.cells + h0, self.half)
        ref = self.table.at[pl.ds(at, rows), :]
        return pltpu.make_async_remote_copy(
            src_ref=ref, dst_ref=ref, send_sem=self.ss.at[i], recv_sem=self.rs.at[i],
            device_id={"fine": to}, device_id_type=MESH)

    def out(self, i):
        p, c, h = self.p, self.p["core"], self.half
        y, yu, yd, yf = p["y"], p["y_up"], p["y_down"], p["y_far"]
        return {
            0: lambda: self.copy(0, p["up"], y, c, 0, h),
            1: lambda: self.copy(1, p["down"], y, c, h, h),
            2: lambda: self.copy(2, p["up"], y, c, h, h),
            3: lambda: self.copy(3, p["down"], y, c, 0, h),
            4: lambda: self.copy(4, p["partner"], y, c, 0, 2 * h),
            5: lambda: self.copy(5, p["up"], yd, c, 0, h),
            6: lambda: self.copy(6, p["down"], yu, c, h, h),
            7: lambda: self.copy(7, p["partner"], yd, c, 0, 2 * h),
            8: lambda: self.copy(8, p["partner"], yu, c, 0, 2 * h),
            9: lambda: self.copy(9, p["partner"], yf, c, 0, 2 * h),
        }[i]()

    def arrival(self, i):
        p, c, h = self.p, self.p["core"], self.half
        y, yu, yd, yf = p["y"], p["y_up"], p["y_down"], p["y_far"]
        o = 1 - c
        spec = {
            0: (yd, c, 0, h), 1: (yu, c, h, h), 2: (yd, c, h, h), 3: (yu, c, 0, h),
            4: (y, o, 0, 2 * h), 5: (yf, c, 0, h), 6: (yf, c, h, h),
            7: (yd, o, 0, 2 * h), 8: (yu, o, 0, 2 * h), 9: (yf, o, 0, 2 * h),
        }[i]
        return self.copy(i, p["partner"], *spec)

    def start(self):
        for i in range(5):
            self.out(i).start()

    def relay(self):
        self.arrival(0).wait_recv()
        self.out(5).start()
        self.arrival(1).wait_recv()
        self.out(6).start()

    def share_near(self):
        self.arrival(2).wait_recv()
        self.out(7).start()
        self.arrival(3).wait_recv()
        self.out(8).start()

    def share_far(self):
        self.arrival(5).wait_recv()
        self.arrival(6).wait_recv()
        self.out(9).start()

    def wait(self, *which):
        for i in which:
            self.arrival(i).wait_recv()

    def drain(self):
        for i in range(10):
            self.out(i).wait_send()


def kernel(
    n_coarse, edge_scale, cell_scale,
    nf, go, cid, halo, es, w1, b1, w2, w3,
    out_gf, out_w1, out_b1, out_w2, out_w3,
    pool_mat, unpool_mat, src_mat, src_mat_t, halo_mat, halo_mat_t,
    es_col, es_row,
    st0, st1, st2, psend, prcv, ysend, yrcv,
    ext, gp, hsend, gret, back, src_feats, wide, acc,
    w_part, w_pair_s, w_pair_r, w_rs_s, w_rs_r, w_y, w_ag, w_fin,
    ps, pr, ys, yr, ags, agr, hs_s, hs_r, ar_s, ar_r,
):
    cells = gp.shape[0] // 8
    group = 8 * cells
    nodes, feat = nf.shape
    edges = K * cells
    side = halo.shape[1]
    rows = group + 2 * side
    g = lax.axis_index("coarse")
    f = lax.axis_index("fine")
    core = lax.rem(f, 2)
    y = lax.div(f, 2)
    y_up, y_far, y_down = lax.rem(y + 1, NY), lax.rem(y + 2, NY), lax.rem(y + 3, NY)
    place = {
        "core": core, "y": y, "y_up": y_up, "y_far": y_far, "y_down": y_down,
        "partner": f + 1 - 2 * core, "up": y_up * 2 + core,
        "down": y_down * 2 + core, "far": y_far * 2 + core,
    }
    right, left = lax.rem(g + 1, n_coarse), lax.rem(g + n_coarse - 1, n_coarse)

    barrier = pltpu.get_barrier_semaphore()
    for name in ("partner", "up", "down", "far"):
        pl.semaphore_signal(barrier, inc=1, device_id={"fine": place[name]}, device_id_type=MESH)

    @pl.loop(1, n_coarse)
    def _(t):
        pl.semaphore_signal(
            barrier, inc=1, device_id={"coarse": lax.rem(g + t, n_coarse)}, device_id_type=MESH)

    own = pl.multiple_of(f * cells, cells)
    y_of = (y, y_up, y_far, y_down)

    def pair_rows(r):
        return pl.multiple_of(y_of[r] * 2 * cells, 2 * cells)

    def build_pool(r):
        ids = lax.broadcasted_iota(I32, (2 * cells, L), 0) + (g * group + y_of[r] * 2 * cells)

        @pl.loop(0, nodes // L)
        def _(b):
            row = cid[pl.ds(b, 1), :]
            pool_mat[r, :, pl.ds(pl.multiple_of(b * L, L), L)] = onehot(ids == row)

    sc = [
        Scatter(place, st, psend.at[i], prcv.at[i], ysend.at[i], yrcv.at[i],
                (ps.at[i], pr.at[i], ys.at[i], yr.at[i]))
        for i, st in enumerate((st0, st1, st2))
    ]
    ag0 = Gather(place, ext, cells, (ags.at[0], agr.at[0]))
    ag1 = Gather(place, gp, cells, (ags.at[1], agr.at[1]))

    def pool(r, x, stage):
        stage[r] = dot(pool_mat[r], x[...])

    build_pool(2)
    pool(2, nf, st0)
    pl.semaphore_wait(barrier, 4 + n_coarse - 1)
    sc[0].emit_pair(2)
    build_pool(1)
    pool(1, nf, st0)
    sc[0].emit_pair(1)
    sc[0].far()
    build_pool(3)
    pool(3, nf, st0)
    sc[0].emit_pair(3)
    sc[0].near_up()
    build_pool(0)
    pool(0, nf, st0)
    sc[0].emit_pair(0)
    sc[0].near_down()
    sc[0].relay()
    for r in (2, 1, 3, 0):
        pool(r, go, st1)
        sc[1].emit_pair(r)

    low, high = sc[0].finish()
    half = cells // 2
    wide[0:half] = low
    wide[half:cells] = high
    ext[pl.ds(own, cells), :] = wide[0:cells].astype(BF16)
    ag0.start()
    sc[1].far()

    at_es = pl.multiple_of(f * (edges // L), edges // L)

    @pl.loop(0, edges // L)
    def _(b):
        es_col[pl.ds(pl.multiple_of(b * L, L), L), :] = columns(es[pl.ds(at_es + b, 1), :])

    lane = lax.broadcasted_iota(I32, (L, L), 1)
    sub = lax.broadcasted_iota(I32, (L, L), 0)
    for k in range(K):
        for q in range(cells // L):
            at = k * cells + q * L
            col = es_col[pl.ds(k + q * L * K, L, stride=K), :]
            es_row[at // L:at // L + 1, :] = jnp.transpose(col)[0:1, :]

            @pl.loop(0, rows // L)
            def _(j, col=col, at=at):
                src_mat[at:at + L, pl.ds(pl.multiple_of(j * L, L), L)] = onehot(col == lane + j * L)

    ag0.relay()
    sc[1].near_up()
    sc[1].near_down()
    for q in range(2):
        col = columns(halo[q:q + 1, :])

        @pl.loop(0, group // L)
        def _(j, col=col, q=q):
            halo_mat[q * L:(q + 1) * L, pl.ds(pl.multiple_of(j * L, L), L)] = onehot(
                col == lane + j * L)
    ag0.share_near()
    sc[1].relay()

    @pl.loop(0, rows // L)
    def _(j):
        at = pl.multiple_of(j * L, L)
        for b in range(edges // L):
            src_mat_t[pl.ds(at, L), b * L:(b + 1) * L] = onehot(es_row[b:b + 1, :] == sub + j * L)

    @pl.loop(0, group // L)
    def _(j):
        at = pl.multiple_of(j * L, L)
        for q in range(2):
            halo_mat_t[pl.ds(at, L), q * L:(q + 1) * L] = onehot(halo[q:q + 1, :] == sub + j * L)

    ag0.share_far()

    low, high = sc[1].finish()
    wide[cells:cells + half] = low
    wide[cells + half:2 * cells] = high
    ag0.wait(4, 7, 8, 9)

    def halo_out(q):
        to, row = (right, 0) if q == 0 else (left, side)
        at = group + row
        return pltpu.make_async_remote_copy(
            src_ref=hsend.at[0, q], dst_ref=ext.at[at:at + side, :],
            send_sem=hs_s.at[q], recv_sem=hs_r.at[q],
            device_id={"coarse": to}, device_id_type=MESH)

    picked = dot(halo_mat[...], ext[0:group, :])
    hsend[0, 0] = picked[0:side].astype(BF16)
    hsend[0, 1] = picked[side:2 * side].astype(BF16)
    halo_out(0).start()
    halo_out(1).start()

    gsum = wide[cells:2 * cells].astype(BF16)
    pooled_bf = wide[0:cells].astype(BF16)
    gnew = dot(gsum, w3[...], ((1,), (1,))).astype(BF16)
    ghid = dot(gnew, w2[...], ((1,), (1,)))
    acc[0:edges, :] = dot(src_mat[:, 0:group], ext[0:group, :])
    pre_dst = dot(pooled_bf, w1[0:feat, :]) + b1[...].astype(F32)
    halo_out(0).wait_recv()
    halo_out(1).wait_recv()
    src_feats[...] = (
        acc[0:edges, :] + dot(src_mat[:, group:rows], ext[group:rows, :])
    ).astype(BF16)

    hsum = jnp.zeros((cells, feat), F32)
    gsum_act = jnp.zeros((cells, feat), F32)
    for k in range(K):
        span = slice(k * cells, (k + 1) * cells)
        pre = pre_dst + dot(src_feats[span, :], w1[feat:2 * feat, :])
        sig = 1.0 / (1.0 + jnp.exp(-pre))
        hsum = hsum + (pre * sig).astype(BF16).astype(F32)
        act = (ghid * sig * (1.0 + pre * (1.0 - sig))).astype(BF16)
        gret[span, :] = act
        gsum_act = gsum_act + act.astype(F32)

    def halo_back(q):
        to = left if q == 0 else right
        return pltpu.make_async_remote_copy(
            src_ref=hsend.at[1, q], dst_ref=back.at[pl.ds(q * side, side), :],
            send_sem=hs_s.at[2 + q], recv_sem=hs_r.at[2 + q],
            device_id={"coarse": to}, device_id_type=MESH)

    outer = dot(src_mat_t[group:rows, :], gret[...])
    hsend[1, 0] = outer[0:side].astype(BF16)
    hsend[1, 1] = outer[side:2 * side].astype(BF16)
    halo_back(0).start()
    halo_back(1).start()

    act_bf = gsum_act.astype(BF16)
    hsum_bf = hsum.astype(BF16)
    new_coarse = (wide[0:cells] + dot(hsum_bf, w2[...])).astype(BF16)
    first = ((0,), (0,))
    w_part[0, 0:feat, 0:feat] = dot(pooled_bf, act_bf, first)
    w_part[0, feat:2 * feat, 0:feat] = dot(src_feats[...], gret[...], first)
    w_part[1, 0:feat, 0:feat] = dot(hsum_bf, gnew, first)
    w_part[1, feat:2 * feat, 0:feat] = dot(new_coarse, gsum, first)
    w_part[:, :, feat:] = jnp.zeros((2, 2 * feat, L), F32)
    bias = jnp.sum(gsum_act, axis=0, keepdims=True)
    for q in range(feat // L):
        w_part[0, q * 16:q * 16 + 1, feat:] = bias[:, q * L:(q + 1) * L]

    pair_w = pltpu.make_async_remote_copy(
        src_ref=w_pair_s, dst_ref=w_pair_r, send_sem=ar_s.at[0], recv_sem=ar_r.at[0],
        device_id={"fine": place["partner"]}, device_id_type=MESH)
    w_pair_s[...] = w_part[1 - core].astype(BF16)
    pair_w.start()

    def spread(r):
        at = pair_rows(r)
        return dot(src_mat_t[pl.ds(at, 2 * cells), :], gret[...])

    for r in (2, 1, 3, 0):
        st2[r] = spread(r)
    halo_back(0).wait_recv()
    halo_back(1).wait_recv()

    def add_back(r):
        at = pair_rows(r)
        st2[r] = st2[r] + dot(halo_mat_t[pl.ds(at, 2 * cells), :], back[...])
        sc[2].emit_pair(r)

    add_back(2)
    add_back(1)
    add_back(3)
    sc[2].far()
    add_back(0)
    sc[2].near_up()
    sc[2].near_down()

    piece = w_rs_s.shape[0] // n_coarse
    pair_w.wait_recv()
    w_rs_s[...] = (w_part[core] + w_pair_r[...].astype(F32)).astype(BF16)

    def piece_out(t):
        j = lax.rem(g + t, n_coarse)
        return pltpu.make_async_remote_copy(
            src_ref=w_rs_s.at[pl.ds(pl.multiple_of(j * piece, piece), piece), :],
            dst_ref=w_rs_r.at[pl.ds(pl.multiple_of((n_coarse - 1 - t) * piece, piece), piece), :],
            send_sem=ar_s.at[1], recv_sem=ar_r.at[1],
            device_id={"coarse": j}, device_id_type=MESH)

    @pl.loop(1, n_coarse)
    def _(t):
        piece_out(t).start()

    sc[2].relay()

    @pl.loop(0, nodes // L)
    def _(b):
        col = columns(cid[pl.ds(b, 1), :])
        at = pl.multiple_of(b * L, L)
        for j in range(group // L):
            unpool_mat[pl.ds(at, L), j * L:(j + 1) * L] = onehot(
                col == lane + (g * group + j * L))

    many = pltpu.make_async_remote_copy(
        src_ref=w_rs_r, dst_ref=w_rs_r, send_sem=ar_s.at[1], recv_sem=ar_r.at[1],
        device_id={"coarse": right}, device_id_type=MESH)
    many.wait_recv()
    my_piece = pl.multiple_of(g * piece, piece)
    total = w_rs_s[pl.ds(my_piece, piece), :].astype(F32)
    for t in range(n_coarse - 1):
        total = total + w_rs_r[t * piece:(t + 1) * piece, :].astype(F32)
    w_y[y] = total.astype(BF16)

    def y_out(t):
        return pltpu.make_async_remote_copy(
            src_ref=w_y.at[y], dst_ref=w_y.at[y], send_sem=ar_s.at[1 + t], recv_sem=ar_r.at[1 + t],
            device_id={"fine": y_of[t] * 2 + core}, device_id_type=MESH)

    def y_in(t):
        src = (y, y_down, y_far, y_up)[t]
        return pltpu.make_async_remote_copy(
            src_ref=w_y.at[src], dst_ref=w_y.at[src], send_sem=ar_s.at[1 + t],
            recv_sem=ar_r.at[1 + t], device_id={"fine": place["up"]}, device_id_type=MESH)

    for t in (1, 2, 3):
        y_out(t).start()

    low, high = sc[2].finish()
    src_grad = jnp.concatenate([low, high], axis=0).astype(BF16)
    last = ((1,), (1,))
    gpool = gnew.astype(F32) + dot(act_bf, w1[0:feat, :], last) + dot(src_grad, w1[feat:, :], last)
    gp[pl.ds(own, cells), :] = gpool.astype(BF16)
    ag1.start()

    for t in (1, 2, 3):
        y_in(t).wait_recv()
    summed = w_y[0].astype(F32)
    for t in range(1, NY):
        summed = summed + w_y[t].astype(F32)
    w_ag[pl.ds(my_piece, piece), :] = summed.astype(BF16)

    def piece_back(t):
        ref = w_ag.at[pl.ds(my_piece, piece), :]
        return pltpu.make_async_remote_copy(
            src_ref=ref, dst_ref=ref, send_sem=ar_s.at[5], recv_sem=ar_r.at[5],
            device_id={"coarse": lax.rem(g + t, n_coarse)}, device_id_type=MESH)

    @pl.loop(1, n_coarse)
    def _(t):
        piece_back(t).start()

    ag1.relay()

    def take(y_at, first_pass):
        at = pl.multiple_of(y_at * 2 * cells, 2 * cells)
        part = dot(unpool_mat[:, pl.ds(at, 2 * cells)], gp[pl.ds(at, 2 * cells), :])
        if first_pass:
            acc[...] = part
        else:
            acc[...] += part

    ag1.wait(4)
    take(y, True)
    ag1.share_near()
    ag1.wait(7)
    take(y_down, False)
    ag1.wait(8)
    take(y_up, False)
    ag1.share_far()

    many_back = pltpu.make_async_remote_copy(
        src_ref=w_rs_r, dst_ref=w_ag.at[0:(n_coarse - 1) * piece, :], send_sem=ar_s.at[5],
        recv_sem=ar_r.at[5], device_id={"coarse": right}, device_id_type=MESH)
    many_back.wait_recv()
    w_fin[core] = w_ag[...]
    pair_fin = pltpu.make_async_remote_copy(
        src_ref=w_ag, dst_ref=w_fin.at[core], send_sem=ar_s.at[6], recv_sem=ar_r.at[6],
        device_id={"fine": place["partner"]}, device_id_type=MESH)
    pair_fin.start()
    ag1.wait(9)
    at_far = pl.multiple_of(y_far * 2 * cells, 2 * cells)

    @pl.loop(0, nodes // (2 * cells))
    def _(b):
        at = pl.ds(pl.multiple_of(b * 2 * cells, 2 * cells), 2 * cells)
        part = dot(unpool_mat[at, pl.ds(at_far, 2 * cells)], gp[pl.ds(at_far, 2 * cells), :])
        out_gf[at, :] = (go[at, :].astype(F32) + (acc[at, :] + part)).astype(BF16)

    pltpu.make_async_remote_copy(
        src_ref=w_ag, dst_ref=w_fin.at[1 - core], send_sem=ar_s.at[6], recv_sem=ar_r.at[6],
        device_id={"fine": place["partner"]}, device_id_type=MESH).wait_recv()
    out_w1[...] = w_fin[0, :, 0:feat].astype(F32) * edge_scale
    out_w2[...] = w_fin[1, 0:feat, 0:feat].astype(F32) * edge_scale
    out_w3[...] = w_fin[1, feat:2 * feat, 0:feat].astype(F32) * cell_scale
    for q in range(feat // L):
        out_b1[:, q * L:(q + 1) * L] = (
            w_fin[0, q * 16:q * 16 + 1, feat:].astype(F32) * edge_scale)

    for s in sc:
        s.drain()
    ag0.drain()
    ag1.drain()
    for q in range(2):
        halo_out(q).wait_send()
        halo_back(q).wait_send()
    pair_w.wait_send()
    many.wait_send()
    for t in (1, 2, 3):
        y_out(t).wait_send()
    many_back.wait_send()
    pair_fin.wait_send()


def local(
    node_feats, grad_out, cluster_ids, halo_lists, edge_sources,
    w_edge_in, b_edge_in, w_edge_out, w_unpool,
):
    nodes, feat = node_feats.shape
    group = edge_sources.shape[0] // K
    cells = group // 8
    edges = K * cells
    side = halo_lists.shape[0] // 2
    rows = group + 2 * side
    n_coarse = lax.axis_size("coarse")
    edge_scale = float(group * n_coarse * K) ** -0.5
    cell_scale = float(group * n_coarse) ** -0.5
    half = cells // 2
    piece = 2 * feat // n_coarse
    wide_feat = feat + L
    vmem = pltpu.VMEM
    dma = pltpu.SemaphoreType.DMA
    out = pl.pallas_call(
        functools.partial(kernel, n_coarse, edge_scale, cell_scale),
        out_shape=(
            jax.ShapeDtypeStruct((nodes, feat), BF16),
            jax.ShapeDtypeStruct((2 * feat, feat), F32),
            jax.ShapeDtypeStruct((1, feat), F32),
            jax.ShapeDtypeStruct((feat, feat), F32),
            jax.ShapeDtypeStruct((feat, feat), F32),
        ),
        in_specs=[pl.BlockSpec(memory_space=vmem)] * 9,
        out_specs=(pl.BlockSpec(memory_space=vmem),) * 5,
        scratch_shapes=[
            vmem((NY, 2 * cells, nodes), BF16),
            vmem((nodes, group), BF16),
            vmem((edges, rows), BF16),
            vmem((rows, edges), BF16),
            vmem((2 * side, group), BF16),
            vmem((group, 2 * side), BF16),
            vmem((edges, L), I32),
            vmem((edges // L, L), I32),
            vmem((NY, 2 * cells, feat), F32),
            vmem((NY, 2 * cells, feat), F32),
            vmem((NY, 2 * cells, feat), F32),
            vmem((3, NY, cells, feat), BF16),
            vmem((3, NY, cells, feat), BF16),
            vmem((3, 6, half, feat), BF16),
            vmem((3, 6, half, feat), BF16),
            vmem((rows, feat), BF16),
            vmem((group, feat), BF16),
            vmem((2, 2, side, feat), BF16),
            vmem((edges, feat), BF16),
            vmem((2 * side, feat), BF16),
            vmem((edges, feat), BF16),
            vmem((2 * cells, feat), F32),
            vmem((nodes, feat), F32),
            vmem((2, 2 * feat, wide_feat), F32),
            vmem((2 * feat, wide_feat), BF16),
            vmem((2 * feat, wide_feat), BF16),
            vmem((2 * feat, wide_feat), BF16),
            vmem(((n_coarse - 1) * piece, wide_feat), BF16),
            vmem((NY, piece, wide_feat), BF16),
            vmem((2 * feat, wide_feat), BF16),
            vmem((2, 2 * feat, wide_feat), BF16),
            dma((3, NY)), dma((3, NY)), dma((3, 6)), dma((3, 6)),
            dma((2, 10)), dma((2, 10)),
            dma((4,)), dma((4,)),
            dma((7,)), dma((7,)),
        ],
        compiler_params=pltpu.CompilerParams(
            collective_id=0, has_side_effects=True, vmem_limit_bytes=60 * 2**20),
    )(
        node_feats, grad_out,
        cluster_ids.reshape(nodes // L, L),
        halo_lists.reshape(2, side),
        edge_sources.reshape(group * K // L, L),
        w_edge_in, b_edge_in.reshape(1, feat), w_edge_out, w_unpool,
    )
    return out[0], out[1], out[2].reshape(feat), out[3], out[4]


def solution(mesh):
    return jax.shard_map(
        local,
        mesh=mesh,
        in_specs=(
            P(("coarse", "fine"), None), P(("coarse", "fine"), None), P(("coarse", "fine")),
            P("coarse"), P("coarse"), P(), P(), P(), P(),
        ),
        out_specs=(P(("coarse", "fine"), None), P(), P(), P(), P()),
        check_vma=False,
    )
```

time: 462 us -> 90.7 us (0.20)
  the two profiles are of different devices: /device:TPU:8 before, /device:TPU:1 now
where the time goes in v1:
time: 90.7 us; the launch traced here: 90.5 us
  Pallas kernels  83.2 us (92%)
  local copies, waits for them, and re-layouts  6.65 us (7%)
    pallas_call x1, Pallas kernels, local(): pl.pallas_call(functools.partial(kernel, n_coarse, edge_scale, cell_scale...  83.2 us
    unnamed x15, local copies, waits for them, and re-layouts  6.08 us

profile of v1, /device:TPU:1, one launch (start us, length us, event | category | flops | bytes accessed | tf_op | source)
XLA Modules:
  0.0 90.5 jit_solution(4657856481908905681)
XLA Ops:
  0.6 0.0 copy-start.4
  0.6 0.6 copy-done.4
  1.3 0.6 reshape.28.b1
  1.9 83.2 %shard_map.128 = (bf16[2048,256]{1,0:T(8,128)(2,1)}, f32[512,256]{1,0:T(8,128)}, f32[1,256]{1,0:T(1,128)}, f32[256,256]{1,0:T(8,128)}, f32[256,256]{1,0:T(8,128)}) custom-call(bf16[2048,256]{1,0:T(8,128)(2,1)} %nf.1, bf16[2048,256]{1,0:T(8,128)(2,1)} %go.1, s32[16,128]{1,0:T(8,128)} %bitcast.5, s32[2,128]{1,0:T(2,128)} %bitcast.6, s32[64,128]{1,0:T(8,128)} %bitcast.4, ...), custom_call_target="tpu_custom_call" | custom-call | tf_op jit(solution)/shard_map/pallas_call | solution.py:558
  85.0 0.0 copy-start
  85.0 2.3 %copy.19 = bf16[2048,256]{1,0:T(8,128)(2,1)} copy(bf16[2048,256]{1,0:T(8,128)(2,1)} %get-tuple-element.20) | data formatting | bytes 2097152
  87.4 0.0 copy-done
  87.4 0.0 copy-start.3
  87.4 0.0 copy-start.2
  87.4 0.8 copy.20
  88.2 0.0 copy-done.3
  88.2 0.6 copy.21
  88.7 0.0 copy-done.2
  88.7 0.0 copy-start.1
  88.7 0.7 copy.22
  89.4 0.3 copy-done.1
  89.8 0.7 copy.23
Async XLA Ops:
  0.6 0.7 copy-start.4
  85.0 2.3 %copy-start = (f32[512,256]{1,0:T(8,128)S(1)}, f32[512,256]{1,0:T(8,128)}, u32[]{:S(2)}) copy-start(f32[512,256]{1,0:T(8,128)} %get-tuple-element.21) | copy-start | bytes 1572868
  87.4 0.8 copy-start.3
  87.4 1.4 %copy-start.2 = (f32[256,256]{1,0:T(8,128)S(1)}, f32[256,256]{1,0:T(8,128)}, u32[]{:S(2)}) copy-start(f32[256,256]{1,0:T(8,128)} %get-tuple-element.23) | copy-start | bytes 786436
  88.7 1.0 %copy-start.1 = (f32[256,256]{1,0:T(8,128)S(1)}, f32[256,256]{1,0:T(8,128)}, u32[]{:S(2)}) copy-start(f32[256,256]{1,0:T(8,128)} %get-tuple-element.24) | copy-start | bytes 786436

commit v2 on v1

v2 whole, which is shorter than its diff:
```python
import functools

import jax
import jax.numpy as jnp
from jax import lax
from jax.experimental import pallas as pl
from jax.experimental.pallas import tpu as pltpu
from jax.sharding import PartitionSpec as P

MESH = pl.DeviceIdType.MESH
F32 = jnp.float32
BF16 = jnp.bfloat16
I32 = jnp.int32
K = 4
NY = 4
L = 128


def dot(a, b, dims=((1,), (0,))):
    return lax.dot_general(a, b, (dims, ((), ())), preferred_element_type=F32)


def onehot(mask):
    return jnp.where(mask, 1.0, 0.0).astype(BF16)


def columns(row):
    return jnp.transpose(jnp.broadcast_to(row, (L, L)))


class Scatter:
    def __init__(self, place, stage, psend, prcv, ysend, yrcv, sems):
        self.p = place
        self.stage, self.psend, self.prcv = stage, psend, prcv
        self.ysend, self.yrcv = ysend, yrcv
        self.ps, self.pr, self.ys, self.yr = sems
        self.cells = psend.shape[1]

    def pair(self, r):
        return pltpu.make_async_remote_copy(
            src_ref=self.psend.at[r], dst_ref=self.prcv.at[r],
            send_sem=self.ps.at[r], recv_sem=self.pr.at[r],
            device_id={"fine": self.p["partner"]}, device_id_type=MESH)

    def ring(self, r):
        return pltpu.make_async_remote_copy(
            src_ref=self.ysend.at[r - 1], dst_ref=self.yrcv.at[r - 1],
            send_sem=self.ys.at[r - 1], recv_sem=self.yr.at[r - 1],
            device_id={"fine": self.p["step"][r]}, device_id_type=MESH)

    def emit_pair(self, r):
        at = pl.multiple_of((1 - self.p["core"]) * self.cells, self.cells)
        self.psend[r] = self.stage[r, pl.ds(at, self.cells), :].astype(BF16)
        self.pair(r).start()

    def chip_sum(self, r):
        self.pair(r).wait_recv()
        at = pl.multiple_of(self.p["core"] * self.cells, self.cells)
        return self.stage[r, pl.ds(at, self.cells), :] + self.prcv[r].astype(F32)

    def send(self, r):
        self.ysend[r - 1] = self.chip_sum(r).astype(BF16)
        self.ring(r).start()

    def finish(self):
        total = self.chip_sum(0)
        for r in (1, 3, 2):
            self.ring(r).wait_recv()
            total = total + self.yrcv[r - 1].astype(F32)
        return total

    def drain(self):
        for r in range(NY):
            self.pair(r).wait_send()
        for r in (1, 2, 3):
            self.ring(r).wait_send()


class Gather:
    def __init__(self, place, table, cells, sems):
        self.p, self.table, self.cells = place, table, cells
        self.ss, self.rs = sems

    def copy(self, i, to, y, core):
        at = pl.multiple_of((y * 2 + core) * self.cells, self.cells)
        ref = self.table.at[pl.ds(at, self.cells), :]
        return pltpu.make_async_remote_copy(
            src_ref=ref, dst_ref=ref, send_sem=self.ss.at[i], recv_sem=self.rs.at[i],
            device_id={"fine": to}, device_id_type=MESH)

    def out(self, i):
        p, c = self.p, self.p["core"]
        if i < NY:
            return self.copy(i, p["step"][i] if i else p["partner"], p["ys"][0], c)
        return self.copy(i, p["partner"], p["ys"][(NY - (i - 3)) % NY], c)

    def arrival(self, i):
        p, c = self.p, self.p["core"]
        if i == 0:
            return self.copy(i, p["partner"], p["ys"][0], 1 - c)
        if i < NY:
            return self.copy(i, p["partner"], p["ys"][NY - i], c)
        return self.copy(i, p["partner"], p["ys"][(NY - (i - 3)) % NY], 1 - c)

    def start(self):
        for i in (2, 1, 3, 0):
            self.out(i).start()

    def share(self, i):
        self.arrival(i).wait_recv()
        self.out(i + 3).start()

    def wait(self, *which):
        for i in which:
            self.arrival(i).wait_recv()

    def drain(self):
        for i in range(7):
            self.out(i).wait_send()


def kernel(
    n_coarse, edge_scale, cell_scale,
    cid, halo, es, b1, nf_hbm, go_hbm, w1_hbm, w2_hbm, w3_hbm,
    out_gf, out_w1, out_b1, out_w2, out_w3,
    nf, go, w1, w2, w3,
    pool_mat, unpool_mat, src_mat, src_mat_t, halo_mat, halo_mat_t,
    es_col, es_row,
    st0, st1, st2, psend, prcv, ysend, yrcv,
    ext, gp, hsend, gret, back, turned, hid, slope, wide, acc,
    w_part, w_pair_s, w_pair_r, w_rs_s, w_rs_r, w_y, w_ag, w_fin, tally,
    ins, ps, pr, ys, yr, ags, agr, hs_s, hs_r, ar_s, ar_r,
):
    cells = gp.shape[0] // 8
    group = 8 * cells
    nodes, feat = nf.shape
    edges = K * cells
    side = halo.shape[1]
    rows = group + 2 * side
    n_bias = feat // L
    g = lax.axis_index("coarse")
    f = lax.axis_index("fine")
    core = lax.rem(f, 2)
    y = lax.div(f, 2)
    y_of = tuple(lax.rem(y + r, NY) for r in range(NY))
    place = {
        "core": core, "ys": y_of, "partner": f + 1 - 2 * core,
        "step": tuple(y_r * 2 + core for y_r in y_of),
    }
    right, left = lax.rem(g + 1, n_coarse), lax.rem(g + n_coarse - 1, n_coarse)

    loads = [
        pltpu.make_async_copy(a, b, ins.at[i])
        for i, (a, b) in enumerate(
            ((nf_hbm, nf), (go_hbm, go), (w1_hbm, w1), (w2_hbm, w2), (w3_hbm, w3)))
    ]
    for load in loads:
        load.start()
    w_ag[:, feat:] = jnp.zeros((2 * feat, L), BF16)

    barrier = pltpu.get_barrier_semaphore()
    for to in (place["partner"],) + place["step"][1:]:
        pl.semaphore_signal(barrier, inc=1, device_id={"fine": to}, device_id_type=MESH)

    @pl.loop(1, n_coarse)
    def _(t):
        pl.semaphore_signal(
            barrier, inc=1, device_id={"coarse": lax.rem(g + t, n_coarse)}, device_id_type=MESH)

    own = pl.multiple_of(f * cells, cells)

    def pair_rows(r):
        return pl.multiple_of(y_of[r] * 2 * cells, 2 * cells)

    def build_pool(r):
        ids = lax.broadcasted_iota(I32, (2 * cells, L), 0) + (g * group + y_of[r] * 2 * cells)

        for b in range(nodes // L):
            pool_mat[r, :, b * L:(b + 1) * L] = onehot(ids == cid[b:b + 1, :])

    sc = [
        Scatter(place, st, psend.at[i], prcv.at[i], ysend.at[i], yrcv.at[i],
                (ps.at[i], pr.at[i], ys.at[i], yr.at[i]))
        for i, st in enumerate((st0, st1, st2))
    ]
    ag0 = Gather(place, ext, cells, (ags.at[0], agr.at[0]))
    ag1 = Gather(place, gp, cells, (ags.at[1], agr.at[1]))

    def pool(r, x, stage):
        stage[r] = dot(pool_mat[r], x[...])

    build_pool(2)
    loads[0].wait()
    pool(2, nf, st0)
    build_pool(1)
    pl.semaphore_wait(barrier, 4 + n_coarse - 1)
    sc[0].emit_pair(2)
    pool(1, nf, st0)
    build_pool(3)
    sc[0].emit_pair(1)
    sc[0].send(2)
    pool(3, nf, st0)
    build_pool(0)
    sc[0].emit_pair(3)
    sc[0].send(1)
    pool(0, nf, st0)
    sc[0].emit_pair(0)
    sc[0].send(3)
    loads[1].wait()
    for r in (2, 1, 3, 0):
        pool(r, go, st1)
        sc[1].emit_pair(r)

    total = sc[0].finish()
    wide[0:cells] = total
    ext[pl.ds(own, cells), :] = total.astype(BF16)
    ag0.start()
    turned[0:feat, :] = jnp.concatenate([jnp.transpose(total.astype(BF16))] * K, axis=1)

    at_es = pl.multiple_of(f * (edges // L), edges // L)

    @pl.loop(0, edges // L)
    def _(b):
        es_col[pl.ds(pl.multiple_of(b * L, L), L), :] = columns(es[pl.ds(at_es + b, 1), :])

    lane = lax.broadcasted_iota(I32, (L, L), 1)
    sub = lax.broadcasted_iota(I32, (L, L), 0)
    for q in range(2):
        col = columns(halo[q:q + 1, :])

        @pl.loop(0, group // L)
        def _(j, col=col, q=q):
            halo_mat[q * L:(q + 1) * L, pl.ds(pl.multiple_of(j * L, L), L)] = onehot(
                col == lane + j * L)

    for k in range(K):
        for q in range(cells // L):
            at = k * cells + q * L
            col = es_col[pl.ds(k + q * L * K, L, stride=K), :]
            es_row[at // L:at // L + 1, :] = jnp.transpose(col)[0:1, :]

            @pl.loop(0, rows // L)
            def _(j, col=col, at=at):
                src_mat[at:at + L, pl.ds(pl.multiple_of(j * L, L), L)] = onehot(col == lane + j * L)

    ag0.share(1)
    ag0.share(3)
    ag0.share(2)
    for r in (2, 1, 3):
        sc[1].send(r)

    @pl.loop(0, group // L)
    def _(j):
        at = pl.multiple_of(j * L, L)
        for q in range(2):
            halo_mat_t[pl.ds(at, L), q * L:(q + 1) * L] = onehot(halo[q:q + 1, :] == sub + j * L)

    ag0.wait(0, 4, 6, 5)

    def halo_out(q):
        to, row = (right, 0) if q == 0 else (left, side)
        at = group + row
        return pltpu.make_async_remote_copy(
            src_ref=hsend.at[0, q], dst_ref=ext.at[at:at + side, :],
            send_sem=hs_s.at[q], recv_sem=hs_r.at[q],
            device_id={"coarse": to}, device_id_type=MESH)

    picked = dot(halo_mat[...], ext[0:group, :])
    hsend[0, 0] = picked[0:side].astype(BF16)
    hsend[0, 1] = picked[side:2 * side].astype(BF16)
    halo_out(0).start()
    halo_out(1).start()

    acc[0:edges, :] = dot(src_mat[:, 0:group], ext[0:group, :])

    @pl.loop(0, rows // L)
    def _(j):
        at = pl.multiple_of(j * L, L)
        for b in range(edges // L):
            src_mat_t[pl.ds(at, L), b * L:(b + 1) * L] = onehot(es_row[b:b + 1, :] == sub + j * L)

    for load in loads[2:]:
        load.wait()
    pooled_bf = wide[0:cells].astype(BF16)
    bias_row = jnp.concatenate([b1[q:q + 1, :].astype(F32) for q in range(n_bias)], axis=1)
    pre_dst = dot(pooled_bf, w1[0:feat, :]) + bias_row
    halo_out(0).wait_recv()
    halo_out(1).wait_recv()
    src_feats = (
        acc[0:edges, :] + dot(src_mat[:, group:rows], ext[group:rows, :])
    ).astype(BF16)
    acc[0:edges, :] = dot(src_feats, w1[feat:2 * feat, :])
    turned[feat:, :] = jnp.transpose(src_feats)

    spans = [slice(k * cells, (k + 1) * cells) for k in range(K)]
    new_coarse = wide[0:cells]
    for span in spans:
        pre = pre_dst + acc[span, :]
        sig = 1.0 / (1.0 + jnp.exp(-pre))
        hidden = (pre * sig).astype(BF16)
        hid[span, :] = hidden
        slope[span, :] = sig * (1.0 + pre * (1.0 - sig))
        new_coarse = new_coarse + dot(hidden, w2[...])
    new_coarse = new_coarse.astype(BF16)

    last = ((1,), (1,))
    gsum = sc[1].finish().astype(BF16)
    gnew = dot(gsum, w3[...], last).astype(BF16)
    ghid = dot(gnew, w2[...], last)
    act_sum = jnp.zeros((cells, feat), F32)
    for span in spans:
        act = (ghid * slope[span, :]).astype(BF16)
        gret[span, :] = act
        act_sum = act_sum + act.astype(F32)

    def halo_back(q):
        to = left if q == 0 else right
        return pltpu.make_async_remote_copy(
            src_ref=hsend.at[1, q], dst_ref=back.at[pl.ds(q * side, side), :],
            send_sem=hs_s.at[2 + q], recv_sem=hs_r.at[2 + q],
            device_id={"coarse": to}, device_id_type=MESH)

    outer = dot(src_mat_t[group:rows, :], gret[...])
    hsend[1, 0] = outer[0:side].astype(BF16)
    hsend[1, 1] = outer[side:2 * side].astype(BF16)
    halo_back(0).start()
    halo_back(1).start()

    w_part[0, :, 0:feat] = dot(turned[...], gret[...])
    gnew_t = jnp.concatenate([jnp.transpose(gnew)] * K, axis=1)
    w_part[1, 0:feat, 0:feat] = jnp.transpose(dot(gnew_t, hid[...]))
    w_part[1, feat:2 * feat, 0:feat] = dot(new_coarse, gsum, ((0,), (0,)))
    w_part[:, :, feat:] = jnp.zeros((2, 2 * feat, L), F32)
    piece = w_rs_s.shape[0] // n_coarse
    bias = jnp.sum(act_sum, axis=0, keepdims=True)
    for q in range(n_bias):
        w_part[0, q * piece:q * piece + 1, feat:] = bias[:, q * L:(q + 1) * L]

    pair_w = pltpu.make_async_remote_copy(
        src_ref=w_pair_s, dst_ref=w_pair_r, send_sem=ar_s.at[0], recv_sem=ar_r.at[0],
        device_id={"fine": place["partner"]}, device_id_type=MESH)
    w_pair_s[...] = w_part[1 - core].astype(BF16)
    pair_w.start()

    def spread(r):
        st2[r] = dot(src_mat_t[pl.ds(pair_rows(r), 2 * cells), :], gret[...])

    spread(2)
    spread(1)
    pair_w.wait_recv()
    w_rs_s[...] = (w_part[core] + w_pair_r[...].astype(F32)).astype(BF16)

    def far_first(i):
        return n_coarse // 2 + (i + 1) // 2 * (1 - 2 * (i % 2))

    def piece_out(t, width):
        j = lax.rem(g + t, n_coarse)
        return pltpu.make_async_remote_copy(
            src_ref=w_rs_s.at[pl.ds(pl.multiple_of(j * piece, piece), piece), 0:width],
            dst_ref=w_rs_r.at[
                pl.ds(pl.multiple_of((n_coarse - 1 - t) * piece, piece), piece), 0:width],
            send_sem=ar_s.at[1], recv_sem=ar_r.at[1],
            device_id={"coarse": j}, device_id_type=MESH)

    @pl.loop(0, n_coarse - 1)
    def _(i):
        t = far_first(i)
        wide_piece = lax.rem(g + t, n_coarse) < n_bias

        @pl.when(wide_piece)
        def _():
            piece_out(t, feat + L).start()

        @pl.when(jnp.logical_not(wide_piece))
        def _():
            piece_out(t, feat).start()

    spread(3)
    spread(0)
    halo_back(0).wait_recv()
    halo_back(1).wait_recv()

    def add_back(r):
        st2[r] = st2[r] + dot(halo_mat_t[pl.ds(pair_rows(r), 2 * cells), :], back[...])
        sc[2].emit_pair(r)

    add_back(2)
    add_back(1)
    sc[2].send(2)
    add_back(3)
    sc[2].send(1)
    add_back(0)
    sc[2].send(3)

    @pl.loop(0, nodes // L)
    def _(b):
        col = columns(cid[pl.ds(b, 1), :])
        at = pl.multiple_of(b * L, L)
        for j in range(group // L):
            unpool_mat[pl.ds(at, L), j * L:(j + 1) * L] = onehot(
                col == lane + (g * group + j * L))

    carries = g < n_bias
    plain = jnp.logical_not(carries)
    n_tiles = 2 * (n_coarse - 1) + n_bias

    def several(width, at):
        ref = w_rs_r.at[:, 0:width]
        return pltpu.make_async_remote_copy(
            src_ref=ref, dst_ref=ref, send_sem=ar_s.at[at], recv_sem=ar_r.at[at],
            device_id={"coarse": right}, device_id_type=MESH)

    def mixed(tiles, at):
        ref = tally.at[0:tiles * piece, :]
        return pltpu.make_async_remote_copy(
            src_ref=ref, dst_ref=ref, send_sem=ar_s.at[at], recv_sem=ar_r.at[at],
            device_id={"coarse": right}, device_id_type=MESH)

    my_piece = pl.multiple_of(g * piece, piece)

    def piece_sum(span):
        total = w_rs_s[pl.ds(my_piece, piece), span].astype(F32)
        for t in range(n_coarse - 1):
            total = total + w_rs_r[t * piece:(t + 1) * piece, span].astype(F32)
        return total

    @pl.when(carries)
    def _():
        several(feat + L, 1).wait_recv()
        w_y[y, :, feat:] = piece_sum(slice(feat, feat + L))

    @pl.when(plain)
    def _():
        several(feat, 1).wait_recv()
        w_y[y, :, feat:] = jnp.zeros((piece, L), F32)

    w_y[y, :, 0:feat] = piece_sum(slice(0, feat))

    def y_copy(t, at):
        return pltpu.make_async_remote_copy(
            src_ref=w_y.at[at], dst_ref=w_y.at[at], send_sem=ar_s.at[1 + t],
            recv_sem=ar_r.at[1 + t], device_id={"fine": place["step"][t]}, device_id_type=MESH)

    for t in (2, 1, 3):
        y_copy(t, y).start()

    gpool = gnew.astype(F32)
    for k in range(K):
        gpool = gpool + dot(gret[k * cells:(k + 1) * cells, :], w1[0:feat, :], last)
    src_grad = sc[2].finish().astype(BF16)
    gpool = gpool + dot(src_grad, w1[feat:, :], last)
    gp[pl.ds(own, cells), :] = gpool.astype(BF16)
    ag1.start()

    def take(y_at, first_pass):
        at = pl.multiple_of(y_at * 2 * cells, 2 * cells)
        part = dot(unpool_mat[:, pl.ds(at, 2 * cells)], gp[pl.ds(at, 2 * cells), :])
        if first_pass:
            acc[...] = part
        else:
            acc[...] += part

    ag1.wait(0)
    take(y, True)

    for t in (1, 2, 3):
        y_copy(t, y_of[NY - t]).wait_recv()
    summed = w_y[0]
    for t in range(1, NY):
        summed = summed + w_y[t]
    w_ag[pl.ds(my_piece, piece), :] = summed.astype(BF16)

    def piece_back(t, width):
        ref = w_ag.at[pl.ds(my_piece, piece), 0:width]
        return pltpu.make_async_remote_copy(
            src_ref=ref, dst_ref=ref, send_sem=ar_s.at[5], recv_sem=ar_r.at[5],
            device_id={"coarse": lax.rem(g + t, n_coarse)}, device_id_type=MESH)

    @pl.when(carries)
    def _():
        @pl.loop(0, n_coarse - 1)
        def _(i):
            piece_back(far_first(i), feat + L).start()

    @pl.when(plain)
    def _():
        @pl.loop(0, n_coarse - 1)
        def _(i):
            piece_back(far_first(i), feat).start()

    ag1.share(1)
    ag1.share(3)
    ag1.share(2)
    ag1.wait(4)
    take(y_of[3], False)
    ag1.wait(6)
    take(y_of[1], False)
    ag1.wait(5)
    at_far = pair_rows(2)

    @pl.loop(0, nodes // (2 * cells))
    def _(b):
        at = pl.ds(pl.multiple_of(b * 2 * cells, 2 * cells), 2 * cells)
        part = dot(unpool_mat[at, pl.ds(at_far, 2 * cells)], gp[pl.ds(at_far, 2 * cells), :])
        out_gf[at, :] = (go[at, :].astype(F32) + (acc[at, :] + part)).astype(BF16)

    @pl.when(carries)
    def _():
        mixed(n_tiles - 1, 5).wait_recv()

    @pl.when(plain)
    def _():
        mixed(n_tiles, 5).wait_recv()

    w_fin[core] = w_ag[...]
    pair_fin = pltpu.make_async_remote_copy(
        src_ref=w_ag, dst_ref=w_fin.at[core], send_sem=ar_s.at[6], recv_sem=ar_r.at[6],
        device_id={"fine": place["partner"]}, device_id_type=MESH)
    pair_fin.start()

    for s in sc:
        s.drain()
    ag0.drain()
    ag1.drain()
    for q in range(2):
        halo_out(q).wait_send()
        halo_back(q).wait_send()
    pair_w.wait_send()

    @pl.when(carries)
    def _():
        mixed(n_tiles - 1, 1).wait_send()
        several(feat + L, 5).wait_send()

    @pl.when(plain)
    def _():
        mixed(n_tiles, 1).wait_send()
        several(feat, 5).wait_send()

    for t in (1, 2, 3):
        y_copy(t, y).wait_send()
    pair_fin.wait_send()
    pltpu.make_async_remote_copy(
        src_ref=w_ag, dst_ref=w_fin.at[1 - core], send_sem=ar_s.at[6], recv_sem=ar_r.at[6],
        device_id={"fine": place["partner"]}, device_id_type=MESH).wait_recv()
    out_w1[...] = w_fin[0, :, 0:feat].astype(F32) * edge_scale
    out_w2[...] = w_fin[1, 0:feat, 0:feat].astype(F32) * edge_scale
    out_w3[...] = w_fin[1, feat:2 * feat, 0:feat].astype(F32) * cell_scale
    for q in range(n_bias):
        out_b1[:, q * L:(q + 1) * L] = (
            w_fin[0, q * piece:q * piece + 1, feat:].astype(F32) * edge_scale)


def store(*refs):
    count = (len(refs) - 1) // 2
    copies = [
        pltpu.make_async_copy(refs[i], refs[count + i], refs[-1].at[i]) for i in range(count)
    ]
    for copy in copies:
        copy.start()
    for copy in copies:
        copy.wait()


def local(
    node_feats, grad_out, cluster_ids, halo_lists, edge_sources,
    w_edge_in, b_edge_in, w_edge_out, w_unpool,
):
    nodes, feat = node_feats.shape
    group = edge_sources.shape[0] // K
    cells = group // 8
    edges = K * cells
    side = halo_lists.shape[0] // 2
    rows = group + 2 * side
    n_coarse = lax.axis_size("coarse")
    edge_scale = float(group * n_coarse * K) ** -0.5
    cell_scale = float(group * n_coarse) ** -0.5
    piece = 2 * feat // n_coarse
    n_tiles = 2 * (n_coarse - 1) + feat // L
    wide_feat = feat + L
    vmem = pltpu.VMEM
    dma = pltpu.SemaphoreType.DMA
    results = (
        ((nodes, feat), BF16), ((2 * feat, feat), F32), ((1, feat), F32),
        ((feat, feat), F32), ((feat, feat), F32),
    )
    in_vmem = pl.BlockSpec(memory_space=vmem)
    anywhere = pl.BlockSpec(memory_space=pl.ANY)
    parts = pl.pallas_call(
        functools.partial(kernel, n_coarse, edge_scale, cell_scale),
        out_shape=tuple(pltpu.VMEM(shape, kind) for shape, kind in results),
        in_specs=[in_vmem] * 4 + [anywhere] * 5,
        out_specs=(in_vmem,) * 5,
        scratch_shapes=[
            vmem((nodes, feat), BF16),
            vmem((nodes, feat), BF16),
            vmem((2 * feat, feat), BF16),
            vmem((feat, feat), BF16),
            vmem((feat, feat), BF16),
            vmem((NY, 2 * cells, nodes), BF16),
            vmem((nodes, group), BF16),
            vmem((edges, rows), BF16),
            vmem((rows, edges), BF16),
            vmem((2 * side, group), BF16),
            vmem((group, 2 * side), BF16),
            vmem((edges, L), I32),
            vmem((edges // L, L), I32),
            vmem((NY, 2 * cells, feat), F32),
            vmem((NY, 2 * cells, feat), F32),
            vmem((NY, 2 * cells, feat), F32),
            vmem((3, NY, cells, feat), BF16),
            vmem((3, NY, cells, feat), BF16),
            vmem((3, 3, cells, feat), BF16),
            vmem((3, 3, cells, feat), BF16),
            vmem((rows, feat), BF16),
            vmem((group, feat), BF16),
            vmem((2, 2, side, feat), BF16),
            vmem((edges, feat), BF16),
            vmem((2 * side, feat), BF16),
            vmem((2 * feat, edges), BF16),
            vmem((edges, feat), BF16),
            vmem((edges, feat), F32),
            vmem((2 * cells, feat), F32),
            vmem((nodes, feat), F32),
            vmem((2, 2 * feat, wide_feat), F32),
            vmem((2 * feat, wide_feat), BF16),
            vmem((2 * feat, wide_feat), BF16),
            vmem((2 * feat, wide_feat), BF16),
            vmem(((n_coarse - 1) * piece, wide_feat), BF16),
            vmem((NY, piece, wide_feat), F32),
            vmem((2 * feat, wide_feat), BF16),
            vmem((2, 2 * feat, wide_feat), BF16),
            vmem((n_tiles * piece, L), BF16),
            dma((5,)),
            dma((3, NY)), dma((3, NY)), dma((3, 3)), dma((3, 3)),
            dma((2, 7)), dma((2, 7)),
            dma((4,)), dma((4,)),
            dma((7,)), dma((7,)),
        ],
        compiler_params=pltpu.CompilerParams(
            collective_id=0, has_side_effects=True, vmem_limit_bytes=58 * 2**20),
    )(
        cluster_ids.reshape(nodes // L, L),
        halo_lists.reshape(2, side),
        edge_sources.reshape(group * K // L, L),
        b_edge_in.reshape(feat // L, L),
        node_feats, grad_out, w_edge_in, w_edge_out, w_unpool,
    )
    out = pl.pallas_call(
        store,
        out_shape=tuple(jax.ShapeDtypeStruct(shape, kind) for shape, kind in results),
        in_specs=[anywhere] * 5,
        out_specs=(anywhere,) * 5,
        scratch_shapes=[dma((5,))],
        compiler_params=pltpu.CompilerParams(vmem_limit_bytes=2**20),
    )(*[pltpu.with_memory_space_constraint(part, pltpu.VMEM) for part in parts])
    return out[0], out[1], out[2].reshape(feat), out[3], out[4]


def solution(mesh):
    return jax.shard_map(
        local,
        mesh=mesh,
        in_specs=(
            P(("coarse", "fine"), None), P(("coarse", "fine"), None), P(("coarse", "fine")),
            P("coarse"), P("coarse"), P(), P(), P(), P(),
        ),
        out_specs=(P(("coarse", "fine"), None), P(), P(), P(), P()),
        check_vma=False,
    )
```

time: 90.7 us -> 71.9 us (0.79)
  Pallas kernels: 83.2 us -> 70.9 us
  local copies, waits for them, and re-layouts: 6.65 us -> 0 us
    pallas_call x1, Pallas kernels: 83.2 us -> 69.5 us  [local(): pl.pallas_call(functools.partial(kernel, n_coarse, edge_scale, cell_scale...]
    unnamed x15 -> x0, local copies, waits for them, and re-layouts: 6.08 us -> none
    pallas_call x0 -> x1, Pallas kernels: none -> 1.36 us  [local(): pl.pallas_call(store, out_shape=tuple((jax.ShapeDtypeStruct(shape, kind)...]
where the time goes in v2:
time: 71.9 us; the launch traced here: 71.7 us
  Pallas kernels  70.9 us (99%)
  between operations  0.8 us (1%)
    pallas_call x1, Pallas kernels, local(): pl.pallas_call(functools.partial(kernel, n_coarse, edge_scale, cell_scale...  69.5 us

profile of v2, /device:TPU:1, one launch (start us, length us, event | category | flops | bytes accessed | tf_op | source)
XLA Modules:
  0.0 71.7 jit_solution(3630475689424358680)
XLA Ops:
  0.6 69.5 %shard_map.128 = (bf16[2048,256]{1,0:T(8,128)(2,1)S(1)}, f32[512,256]{1,0:T(8,128)S(1)}, f32[1,256]{1,0:T(1,128)S(1)}, f32[256,256]{1,0:T(8,128)S(1)}, f32[256,256]{1,0:T(8,128)S(1)}) custom-call(s32[16,128]{1,0:T(8,128)} %bitcast.6, s32[2,128]{1,0:T(2,128)} %bitcast.7, s32[64,128]{1,0:T(8,128)} %bitcast.5, bf16[2,128]{1,0:T(2,128)(2,1)} %bitcast.8, ...), custom_call_target="tpu_custom_call" | custom-call | tf_op jit(solution)/shard_map/pallas_call | solution.py:589
  70.2 1.4 %shard_map.129 = (bf16[2048,256]{1,0:T(8,128)(2,1)}, f32[512,256]{1,0:T(8,128)}, f32[1,256]{1,0:T(1,128)}, f32[256,256]{1,0:T(8,128)}, f32[256,256]{1,0:T(8,128)}) custom-call(bf16[2048,256]{1,0:T(8,128)(2,1)S(1)} %get-tuple-element.15.refs_0_, f32[512,256]{1,0:T(8,128)S(1)} %get-tuple-element.16.refs_1_, f32[1,256]{1,0:T(1,128)S(1)} %get-tuple-element.17.refs_2_, ...), custom_call_target="tpu_custom_call" | custom-call | tf_op jit(solution)/shard_map/pallas_call | solution.py:649

commit v3 on v2

v3 whole, which is shorter than its diff:
```python
import functools

import jax
import jax.numpy as jnp
from jax import lax
from jax.experimental import pallas as pl
from jax.experimental.pallas import tpu as pltpu
from jax.sharding import PartitionSpec as P

MESH = pl.DeviceIdType.MESH
F32 = jnp.float32
BF16 = jnp.bfloat16
I32 = jnp.int32
K = 4
NY = 4
L = 128


def dot(a, b, dims=((1,), (0,))):
    return lax.dot_general(a, b, (dims, ((), ())), preferred_element_type=F32)


def onehot(mask):
    return jnp.where(mask, 1.0, 0.0).astype(BF16)


def onehot16(mask):
    return jnp.where(mask, jnp.ones((), BF16), jnp.zeros((), BF16))


def columns(row):
    return jnp.transpose(jnp.broadcast_to(row, (L, L)))


class Scatter:
    def __init__(self, place, stage, psend, prcv, ysend, yrcv, sems, lots=1):
        self.p = place
        self.stage, self.psend, self.prcv = stage, psend, prcv
        self.ysend, self.yrcv = ysend, yrcv
        self.ps, self.pr, self.ys, self.yr = sems
        self.cells = psend.shape[1]
        self.lots, self.rows = lots, psend.shape[1] // lots

    def part(self, q):
        return pl.ds(q * self.rows, self.rows)

    def pair(self, r, q):
        return pltpu.make_async_remote_copy(
            src_ref=self.psend.at[r, self.part(q)], dst_ref=self.prcv.at[r, self.part(q)],
            send_sem=self.ps.at[r, q], recv_sem=self.pr.at[r, q],
            device_id={"fine": self.p["partner"]}, device_id_type=MESH)

    def ring(self, r, q):
        return pltpu.make_async_remote_copy(
            src_ref=self.ysend.at[r - 1, self.part(q)], dst_ref=self.yrcv.at[r - 1, self.part(q)],
            send_sem=self.ys.at[r - 1, q], recv_sem=self.yr.at[r - 1, q],
            device_id={"fine": self.p["step"][r]}, device_id_type=MESH)

    def emit_pair(self, r):
        at = pl.multiple_of((1 - self.p["core"]) * self.cells, self.cells)
        self.psend[r] = self.stage[r, pl.ds(at, self.cells), :].astype(BF16)
        for q in range(self.lots):
            self.pair(r, q).start()

    def chip_sum(self, r, q):
        self.pair(r, q).wait_recv()
        at = pl.multiple_of(self.p["core"] * self.cells + q * self.rows, self.rows)
        return self.stage[r, pl.ds(at, self.rows), :] + self.prcv[r, self.part(q)].astype(F32)

    def send(self, r, q=0):
        self.ysend[r - 1, self.part(q)] = self.chip_sum(r, q).astype(BF16)
        self.ring(r, q).start()

    def finish(self, q=0):
        total = self.chip_sum(0, q)
        for r in (1, 3, 2):
            self.ring(r, q).wait_recv()
            total = total + self.yrcv[r - 1, self.part(q)].astype(F32)
        return total

    def drain(self):
        for q in range(self.lots):
            for r in range(NY):
                self.pair(r, q).wait_send()
            for r in (1, 2, 3):
                self.ring(r, q).wait_send()


class Gather:
    def __init__(self, place, table, cells, sems, lots=1):
        self.p, self.table, self.cells = place, table, cells
        self.lots, self.rows = lots, cells // lots
        self.ss, self.rs = sems

    def copy(self, i, q, to, y, core):
        at = pl.multiple_of((y * 2 + core) * self.cells + q * self.rows, self.rows)
        ref = self.table.at[pl.ds(at, self.rows), :]
        return pltpu.make_async_remote_copy(
            src_ref=ref, dst_ref=ref, send_sem=self.ss.at[i, q], recv_sem=self.rs.at[i, q],
            device_id={"fine": to}, device_id_type=MESH)

    def out(self, i, q):
        p, c = self.p, self.p["core"]
        if i < NY:
            return self.copy(i, q, p["step"][i] if i else p["partner"], p["ys"][0], c)
        return self.copy(i, q, p["partner"], p["ys"][(NY - (i - 3)) % NY], c)

    def arrival(self, i, q):
        p, c = self.p, self.p["core"]
        if i == 0:
            return self.copy(i, q, p["partner"], p["ys"][0], 1 - c)
        if i < NY:
            return self.copy(i, q, p["partner"], p["ys"][NY - i], c)
        return self.copy(i, q, p["partner"], p["ys"][(NY - (i - 3)) % NY], 1 - c)

    def start(self, q=0):
        for i in (2, 1, 3, 0):
            self.out(i, q).start()

    def share(self, i, q=0):
        self.arrival(i, q).wait_recv()
        self.out(i + 3, q).start()

    def wait(self, *which):
        for q in range(self.lots):
            for i in which:
                self.arrival(i, q).wait_recv()

    def drain(self):
        for q in range(self.lots):
            for i in range(7):
                self.out(i, q).wait_send()


def kernel(
    n_coarse, nx, edge_scale, cell_scale,
    cid_hbm, halo_hbm, es_hbm, b1_hbm, nf_hbm, go_hbm, w1_hbm, w2_hbm, w3_hbm,
    out_gf, out_w1, out_b1, out_w2, out_w3,
    cid, halo, es, b1, nf, go, w1, w2, w3,
    pool_mat, unpool_mat, src_mat, src_mat_t, halo_mat, list_mat,
    es_col, es_row,
    st0, st1, st2, psend, prcv, ysend, yrcv,
    st3, psend3, prcv3, ysend3, yrcv3, hb,
    ext, gp, hsend, gret, back, turned, hid, slope, wide, acc,
    w_part, w_pair_s, w_pair_r, w_rs, w_x, w_own, w_z_s, w_z_r, w_y, w_ag, w_fin,
    b_pair_s, b_pair_r, b_x, b_z, b_y,
    ins, ps, pr, ys, yr, ags, agr, hs_s, hs_r, ar_s, ar_r, br_s, br_r,
):
    cells = gp.shape[0] // 8
    group = 8 * cells
    nodes, feat = nf.shape
    edges = K * cells
    side = halo.shape[1]
    rows = group + 2 * side
    n_bias = feat // L
    g = lax.axis_index("coarse")
    f = lax.axis_index("fine")
    core = lax.rem(f, 2)
    y = lax.div(f, 2)
    y_of = tuple(lax.rem(y + r, NY) for r in range(NY))
    place = {
        "core": core, "ys": y_of, "partner": f + 1 - 2 * core,
        "step": tuple(y_r * 2 + core for y_r in y_of),
    }
    right, left = lax.rem(g + 1, n_coarse), lax.rem(g + n_coarse - 1, n_coarse)

    nz = n_coarse // nx
    z, x = lax.div(g, nx), lax.rem(g, nx)
    x_peer = [z * nx + lax.rem(x + d, nx) for d in range(nx)]
    z_peer = [lax.rem(z + d, nz) * nx + x for d in range(nz)]

    quarter = nodes // 4
    first_loads = [pltpu.make_async_copy(cid_hbm, cid, ins.at[4])] + [
        pltpu.make_async_copy(
            nf_hbm.at[pl.ds(i * quarter, quarter), :], nf.at[pl.ds(i * quarter, quarter), :],
            ins.at[5 + i])
        for i in range(4)
    ]
    for load in first_loads:
        load.start()
    barrier = pltpu.get_barrier_semaphore()
    fine_peers = (place["partner"],) + place["step"][1:]
    coarse_peers = [right, left] + x_peer[1:] + z_peer[1:]
    for to in fine_peers:
        pl.semaphore_signal(barrier, inc=1, device_id={"fine": to}, device_id_type=MESH)
    for to in coarse_peers:
        pl.semaphore_signal(barrier, inc=1, device_id={"coarse": to}, device_id_type=MESH)
    loads = [
        pltpu.make_async_copy(a, b, ins.at[i])
        for i, (a, b) in enumerate(
            ((go_hbm, go), (w1_hbm, w1), (w2_hbm, w2), (w3_hbm, w3)))
    ] + [
        pltpu.make_async_copy(a, b, ins.at[9 + i])
        for i, (a, b) in enumerate(((halo_hbm, halo), (es_hbm, es), (b1_hbm, b1)))
    ]
    for load in loads:
        load.start()

    own = pl.multiple_of(f * cells, cells)

    def pair_rows(r):
        return pl.multiple_of(y_of[r] * 2 * cells, 2 * cells)

    cell_ids = lax.broadcasted_iota(I32, (2 * cells, L), 0).astype(jnp.int16)

    def build_pool(r):
        base = g * group + y_of[r] * 2 * cells
        for b in range(nodes // L):
            row = jnp.broadcast_to(cid[b:b + 1, :] - base, (16, L)).astype(jnp.int16)
            pool_mat[r, :, b * L:(b + 1) * L] = onehot16(
                cell_ids == jnp.concatenate([row] * (2 * cells // 16), axis=0))

    sc = [
        Scatter(place, st, psend.at[i], prcv.at[i], ysend.at[i], yrcv.at[i],
                (ps.at[i], pr.at[i], ys.at[i], yr.at[i]), 1 if i == 1 else 2)
        for i, st in enumerate((st0, st1, st2))
    ]
    sc.append(Scatter(place, st3, psend3, prcv3, ysend3, yrcv3,
                      (ps.at[3], pr.at[3], ys.at[3], yr.at[3])))
    ag0 = Gather(place, ext, cells, (ags.at[0], agr.at[0]), 2)
    ag1 = Gather(place, gp, cells, (ags.at[1], agr.at[1]), 2)
    share = hb.shape[0] // 8
    ag2 = Gather(place, hb, share, (ags.at[2], agr.at[2]))

    def pool(r, x, stage):
        stage[r] = dot(pool_mat[r], x[...])

    first_loads[0].wait()
    build_pool(2)
    for load in first_loads[1:]:
        load.wait()
    pool(2, nf, st0)
    pl.semaphore_wait(barrier, len(fine_peers) + len(coarse_peers))
    sc[0].emit_pair(2)
    build_pool(1)
    pool(1, nf, st0)
    sc[0].emit_pair(1)
    sc[0].send(2, 0)
    build_pool(3)
    pool(3, nf, st0)
    sc[0].emit_pair(3)
    sc[0].send(1, 0)
    build_pool(0)
    pool(0, nf, st0)
    sc[0].emit_pair(0)
    sc[0].send(3, 0)
    for r in (2, 1, 3):
        sc[0].send(r, 1)
    loads[0].wait()
    pool(2, go, st1)
    sc[1].emit_pair(2)
    pool(1, go, st1)
    sc[1].emit_pair(1)
    half = cells // 2

    def pooled_half(q):
        total = sc[0].finish(q)
        wide[q * half:(q + 1) * half] = total
        at = pl.multiple_of(own + q * half, half)
        ext[pl.ds(at, half), :] = total.astype(BF16)
        ag0.start(q)

    pooled_half(0)
    for r in (3, 0):
        pool(r, go, st1)
        sc[1].emit_pair(r)
    pooled_half(1)
    turned[0:feat, :] = jnp.concatenate(
        [jnp.transpose(wide[0:cells].astype(BF16))] * K, axis=1)

    for load in loads[1:]:
        load.wait()
    at_es = pl.multiple_of(f * (edges // L), edges // L)

    @pl.loop(0, edges // L)
    def _(b):
        es_col[pl.ds(pl.multiple_of(b * L, L), L), :] = columns(es[pl.ds(at_es + b, 1), :])

    lane = lax.broadcasted_iota(I32, (L, L), 1)
    sub = lax.broadcasted_iota(I32, (L, L), 0)
    for q in range(2):
        col = columns(halo[q:q + 1, :])

        @pl.loop(0, group // L)
        def _(j, col=col, q=q):
            halo_mat[q * L:(q + 1) * L, pl.ds(pl.multiple_of(j * L, L), L)] = onehot(
                col == lane + j * L)

    for k in range(K):
        for q in range(cells // L):
            at = k * cells + q * L
            col = es_col[pl.ds(k + q * L * K, L, stride=K), :]
            es_row[at // L:at // L + 1, :] = jnp.transpose(col)[0:1, :]

            @pl.loop(0, rows // L)
            def _(j, col=col, at=at):
                src_mat[at:at + L, pl.ds(pl.multiple_of(j * L, L), L)] = onehot(col == lane + j * L)

    for r in (1, 3, 2):
        ag0.share(r, 0)
    for r in (1, 3, 2):
        ag0.share(r, 1)
    for r in (2, 1, 3):
        sc[1].send(r)

    ag0.wait(0, 4, 6, 5)

    def halo_out(q):
        to, row = (right, 0) if q == 0 else (left, side)
        at = group + row
        return pltpu.make_async_remote_copy(
            src_ref=hsend.at[0, q], dst_ref=ext.at[at:at + side, :],
            send_sem=hs_s.at[q], recv_sem=hs_r.at[q],
            device_id={"coarse": to}, device_id_type=MESH)

    picked = dot(halo_mat[...], ext[0:group, :])
    hsend[0, 0] = picked[0:side].astype(BF16)
    hsend[0, 1] = picked[side:2 * side].astype(BF16)
    halo_out(0).start()
    halo_out(1).start()

    acc[0:edges, :] = dot(src_mat[:, 0:group], ext[0:group, :])

    @pl.loop(0, rows // L)
    def _(j):
        at = pl.multiple_of(j * L, L)
        for b in range(edges // L):
            src_mat_t[pl.ds(at, L), b * L:(b + 1) * L] = onehot(es_row[b:b + 1, :] == sub + j * L)

    pooled_bf = wide[0:cells].astype(BF16)
    bias_row = jnp.concatenate([b1[q:q + 1, :].astype(F32) for q in range(n_bias)], axis=1)
    pre_dst = dot(pooled_bf, w1[0:feat, :]) + bias_row
    halo_out(0).wait_recv()
    halo_out(1).wait_recv()
    src_feats = (
        acc[0:edges, :] + dot(src_mat[:, group:rows], ext[group:rows, :])
    ).astype(BF16)
    acc[0:edges, :] = dot(src_feats, w1[feat:2 * feat, :])
    turned[feat:, :] = jnp.transpose(src_feats)

    spans = [slice(k * cells, (k + 1) * cells) for k in range(K)]
    new_coarse = wide[0:cells]
    for span in spans:
        pre = pre_dst + acc[span, :]
        sig = 1.0 / (1.0 + jnp.exp(-pre))
        hidden = (pre * sig).astype(BF16)
        hid[span, :] = hidden
        slope[span, :] = sig * (1.0 + pre * (1.0 - sig))
        new_coarse = new_coarse + dot(hidden, w2[...])
    new_coarse = new_coarse.astype(BF16)

    def spread(r):
        st2[r] = dot(src_mat_t[pl.ds(pair_rows(r), 2 * cells), :], gret[...])
        sc[2].emit_pair(r)

    last = ((1,), (1,))
    gsum = sc[1].finish().astype(BF16)
    gnew = dot(gsum, w3[...], last).astype(BF16)
    ghid = dot(gnew, w2[...], last)
    act_sum = jnp.zeros((cells, feat), F32)
    for span in spans:
        act = (ghid * slope[span, :]).astype(BF16)
        gret[span, :] = act
        act_sum = act_sum + act.astype(F32)


    def halo_back(q):
        to = left if q == 0 else right
        return pltpu.make_async_remote_copy(
            src_ref=hsend.at[1, q], dst_ref=back.at[pl.ds(q * side, side), :],
            send_sem=hs_s.at[2 + q], recv_sem=hs_r.at[2 + q],
            device_id={"coarse": to}, device_id_type=MESH)

    w_part[0] = dot(turned[...], gret[...])
    gnew_t = jnp.concatenate([jnp.transpose(gnew)] * K, axis=1)
    w_part[1, 0:feat, :] = jnp.transpose(dot(gnew_t, hid[...]))
    w_part[1, feat:2 * feat, :] = dot(new_coarse, gsum, ((0,), (0,)))
    b_pair_s[...] = jnp.zeros_like(b_pair_s)
    bias = jnp.sum(act_sum, axis=0, keepdims=True)
    for q in range(n_bias):
        b_pair_s[q:q + 1, :] = bias[:, q * L:(q + 1) * L]

    def remote(src, dst, i, to, sems=(ar_s, ar_r)):
        return pltpu.make_async_remote_copy(
            src_ref=src, dst_ref=dst, send_sem=sems[0].at[i], recv_sem=sems[1].at[i],
            device_id=to, device_id_type=MESH)

    small = (br_s, br_r)
    partner = {"fine": place["partner"]}
    pair_w = remote(w_pair_s, w_pair_r, 0, partner)
    pair_b = remote(b_pair_s, b_pair_r, 0, partner, small)
    w_pair_s[...] = w_part[1 - core].astype(BF16)
    pair_w.start()
    pair_b.start()

    spread(2)
    spread(1)

    piece = 2 * feat // n_coarse
    far = sorted(range(nz), key=lambda d: (-min(d, nz - d), d))
    near = sorted(range(nz), key=lambda d: (min(d, nz - d), d))
    lot = nz // 2
    pair_w.wait_recv()
    for i in range(nx):
        for p in range(nz):
            at = pl.multiple_of((i * nz + lax.rem(z + far[p], nz)) * piece, piece)
            w_rs[i, p] = (
                w_part[core, pl.ds(at, piece), :] + w_pair_r[pl.ds(at, piece), :].astype(F32)
            ).astype(BF16)

    def x_copy(d, h):
        part = pl.ds(h * lot, lot)
        return remote(w_rs.at[lax.rem(x + d, nx), part], w_x.at[d - 1, part],
                      1 + h * (nx - 1) + d - 1, {"coarse": x_peer[d]})

    def z_copy(p):
        return remote(w_z_s.at[p], w_z_r.at[p], 7 + p, {"coarse": z_peer[far[p]]})

    def bx_copy(d, at):
        return remote(b_x.at[at], b_x.at[at], d, {"coarse": x_peer[d]}, small)

    def bz_copy(d, at):
        return remote(b_z.at[at], b_z.at[at], 3 + d, {"coarse": z_peer[d]}, small)

    def by_copy(t, at):
        return remote(b_y.at[at], b_y.at[at], 10 + t, {"fine": place["step"][t]}, small)

    for h in range(2):
        for d in range(1, nx):
            x_copy(d, h).start()
    outer = dot(src_mat_t[group:rows, :], gret[...])
    hsend[1, 0] = outer[0:side].astype(BF16)
    hsend[1, 1] = outer[side:2 * side].astype(BF16)
    halo_back(0).start()
    halo_back(1).start()
    pair_b.wait_recv()
    b_x[x] = b_pair_s[...] + b_pair_r[...]
    for d in range(1, nx):
        bx_copy(d, x).start()

    spread(3)
    spread(0)
    for q in range(2):
        for r in (2, 1, 3):
            sc[2].send(r, q)

    for h in range(2):
        for d in range(1, nx):
            x_copy(d, h).wait_recv()
        for p in range(h * lot, (h + 1) * lot):
            total = w_rs[x, p].astype(F32)
            for d in range(1, nx):
                total = total + w_x[d - 1, p].astype(F32)
            if p < nz - 1:
                w_z_s[p] = total.astype(BF16)
                z_copy(p).start()
            else:
                w_own[...] = total
    for d in range(1, nx):
        bx_copy(d, lax.rem(x + nx - d, nx)).wait_recv()
    total = b_x[0]
    for i in range(1, nx):
        total = total + b_x[i]
    b_z[z] = total
    for d in range(1, nz):
        bz_copy(d, z).start()

    halo_back(0).wait_recv()
    halo_back(1).wait_recv()
    for r in (2, 1, 3, 0):
        at = pl.multiple_of(y_of[r] * 2 * share, 2 * share)
        st3[r] = back[pl.ds(at, 2 * share), :].astype(F32)
        sc[3].emit_pair(r)

    @pl.loop(0, nodes // L)
    def _(b):
        col = columns(cid[pl.ds(b, 1), :])
        at = pl.multiple_of(b * L, L)
        for j in range(group // L):
            unpool_mat[pl.ds(at, L), j * L:(j + 1) * L] = onehot(
                col == lane + (g * group + j * L))
        for q in range(2):
            list_mat[pl.ds(at, L), q * L:(q + 1) * L] = onehot(
                col == halo[q:q + 1, :] + g * group)

    for r in (2, 1, 3):
        sc[3].send(r)
    gpool = gnew.astype(F32)
    for k in range(K):
        gpool = gpool + dot(gret[k * cells:(k + 1) * cells, :], w1[0:feat, :], last)

    total = w_own[...]
    for p in range(nz - 1):
        z_copy(p).wait_recv()
        total = total + w_z_r[p].astype(F32)
    w_y[y] = total

    def y_copy(t, at):
        return remote(w_y.at[at], w_y.at[at], 14 + t, {"fine": place["step"][t]})

    for t in (2, 1, 3):
        y_copy(t, y).start()
    for d in range(1, nz):
        bz_copy(d, lax.rem(z + nz - d, nz)).wait_recv()
    total = b_z[0]
    for i in range(1, nz):
        total = total + b_z[i]
    b_y[y] = total
    for t in (2, 1, 3):
        by_copy(t, y).start()

    for q in range(2):
        src_grad = dot(sc[2].finish(q).astype(BF16), w1[feat:, :], last)
        at = pl.multiple_of(own + q * half, half)
        gp[pl.ds(at, half), :] = (gpool[q * half:(q + 1) * half] + src_grad).astype(BF16)
        ag1.start(q)
    returned = dot(sc[3].finish().astype(BF16), w1[feat:, :], last)
    hb[pl.ds(pl.multiple_of(f * share, share), share), :] = returned.astype(BF16)
    ag2.start()

    def take(y_at, first_pass):
        at = pl.multiple_of(y_at * 2 * cells, 2 * cells)
        part = dot(unpool_mat[:, pl.ds(at, 2 * cells)], gp[pl.ds(at, 2 * cells), :])
        if first_pass:
            acc[...] = part
        else:
            acc[...] += part

    for t in (1, 2, 3):
        y_copy(t, y_of[NY - t]).wait_recv()
    summed = w_y[0]
    for t in range(1, NY):
        summed = summed + w_y[t]
    w_ag[x, 0] = summed.astype(BF16)

    def z_back(d):
        return remote(w_ag.at[x, 0], w_ag.at[x, near.index((nz - d) % nz)],
                      17 + near.index((nz - d) % nz), {"coarse": z_peer[d]})

    def z_here(q):
        ref = w_ag.at[x, q]
        return remote(ref, ref, 17 + q, {"coarse": z_peer[1]})

    def x_back(d, h, at):
        ref = w_ag.at[at, pl.ds(h * lot, lot)]
        return remote(ref, ref, 25 + h * (nx - 1) + d - 1, {"coarse": x_peer[d]})

    for d in far[:-1]:
        z_back(d).start()
    ag1.wait(0)
    take(y, True)

    def forward(h):
        for q in range(max(1, h * lot), (h + 1) * lot):
            z_here(q).wait_recv()
        for d in range(1, nx):
            x_back(d, h, x).start()

    forward(0)
    for q in range(2):
        for r in (1, 3, 2):
            ag1.share(r, q)
    for r in (1, 3, 2):
        ag2.share(r)
    forward(1)
    ag1.wait(4)
    take(y_of[3], False)
    ag1.wait(6)
    take(y_of[1], False)
    ag2.wait(0, 4, 6, 5)
    acc[...] += dot(list_mat[...], hb[...])
    ag1.wait(5)
    at_far = pair_rows(2)

    @pl.loop(0, nodes // (2 * cells))
    def _(b):
        at = pl.ds(pl.multiple_of(b * 2 * cells, 2 * cells), 2 * cells)
        part = dot(unpool_mat[at, pl.ds(at_far, 2 * cells)], gp[pl.ds(at_far, 2 * cells), :])
        out_gf[at, :] = (go[at, :].astype(F32) + (acc[at, :] + part)).astype(BF16)

    for h in range(2):
        for d in range(1, nx):
            x_back(d, h, lax.rem(x + nx - d, nx)).wait_recv()
    pair_fin = remote(w_ag, w_fin.at[core], 31, partner)
    pair_fin.start()
    w_fin[core] = w_ag[...]
    for t in (1, 2, 3):
        by_copy(t, y_of[NY - t]).wait_recv()
    total = b_y[0]
    for t in range(1, NY):
        total = total + b_y[t]
    for q in range(n_bias):
        out_b1[:, q * L:(q + 1) * L] = total[q:q + 1, :] * edge_scale

    def emit(h):
        for i in range(nx):
            for q in range(nz):
                at = lax.rem(z + near[q], nz) * piece
                value = w_fin[h, i, q].astype(F32)
                if h == 0:
                    here = pl.ds(pl.multiple_of(i * nz * piece + at, piece), piece)
                    out_w1[here, :] = value * edge_scale
                elif i < nx // 2:
                    here = pl.ds(pl.multiple_of(i * nz * piece + at, piece), piece)
                    out_w2[here, :] = value * edge_scale
                else:
                    here = pl.ds(pl.multiple_of((i - nx // 2) * nz * piece + at, piece), piece)
                    out_w3[here, :] = value * cell_scale

    @pl.when(core == 0)
    def _():
        emit(0)

    @pl.when(core == 1)
    def _():
        emit(1)

    for s in sc:
        s.drain()
    ag0.drain()
    ag1.drain()
    ag2.drain()
    for q in range(2):
        halo_out(q).wait_send()
        halo_back(q).wait_send()
    pair_w.wait_send()
    pair_b.wait_send()
    for h in range(2):
        for d in range(1, nx):
            x_copy(d, h).wait_send()
            x_back(d, h, x).wait_send()
    for d in range(1, nx):
        bx_copy(d, x).wait_send()
    for p in range(nz - 1):
        z_copy(p).wait_send()
    for d in range(1, nz):
        bz_copy(d, z).wait_send()
        z_back(d).wait_send()
    for t in (1, 2, 3):
        y_copy(t, y).wait_send()
        by_copy(t, y).wait_send()
    pair_fin.wait_send()
    remote(w_ag, w_fin.at[1 - core], 31, partner).wait_recv()

    @pl.when(core == 0)
    def _():
        emit(1)

    @pl.when(core == 1)
    def _():
        emit(0)


def store(*refs):
    count = (len(refs) - 1) // 2
    copies = [
        pltpu.make_async_copy(refs[i], refs[count + i], refs[-1].at[i]) for i in range(count)
    ]
    for copy in copies:
        copy.start()
    for copy in copies:
        copy.wait()


def local(
    node_feats, grad_out, cluster_ids, halo_lists, edge_sources,
    w_edge_in, b_edge_in, w_edge_out, w_unpool,
):
    nodes, feat = node_feats.shape
    group = edge_sources.shape[0] // K
    cells = group // 8
    edges = K * cells
    side = halo_lists.shape[0] // 2
    rows = group + 2 * side
    n_coarse = lax.axis_size("coarse")
    edge_scale = float(group * n_coarse * K) ** -0.5
    cell_scale = float(group * n_coarse) ** -0.5
    share = 2 * side // 8
    piece = 2 * feat // n_coarse
    nx = 4 if n_coarse > 4 else 2
    nz = n_coarse // nx
    vmem = pltpu.VMEM
    dma = pltpu.SemaphoreType.DMA
    results = (
        ((nodes, feat), BF16), ((2 * feat, feat), F32), ((1, feat), F32),
        ((feat, feat), F32), ((feat, feat), F32),
    )
    in_vmem = pl.BlockSpec(memory_space=vmem)
    anywhere = pl.BlockSpec(memory_space=pl.ANY)
    parts = pl.pallas_call(
        functools.partial(kernel, n_coarse, nx, edge_scale, cell_scale),
        out_shape=tuple(pltpu.VMEM(shape, kind) for shape, kind in results),
        in_specs=[anywhere] * 9,
        out_specs=(in_vmem,) * 5,
        scratch_shapes=[
            vmem((nodes // L, L), I32),
            vmem((2, side), I32),
            vmem((group * K // L, L), I32),
            vmem((feat // L, L), BF16),
            vmem((nodes, feat), BF16),
            vmem((nodes, feat), BF16),
            vmem((2 * feat, feat), BF16),
            vmem((feat, feat), BF16),
            vmem((feat, feat), BF16),
            vmem((NY, 2 * cells, nodes), BF16),
            vmem((nodes, group), BF16),
            vmem((edges, rows), BF16),
            vmem((rows, edges), BF16),
            vmem((2 * side, group), BF16),
            vmem((nodes, 2 * side), BF16),
            vmem((edges, L), I32),
            vmem((edges // L, L), I32),
            vmem((NY, 2 * cells, feat), F32),
            vmem((NY, 2 * cells, feat), F32),
            vmem((NY, 2 * cells, feat), F32),
            vmem((3, NY, cells, feat), BF16),
            vmem((3, NY, cells, feat), BF16),
            vmem((3, 3, cells, feat), BF16),
            vmem((3, 3, cells, feat), BF16),
            vmem((NY, 2 * share, feat), F32),
            vmem((NY, share, feat), BF16),
            vmem((NY, share, feat), BF16),
            vmem((3, share, feat), BF16),
            vmem((3, share, feat), BF16),
            vmem((2 * side, feat), BF16),
            vmem((rows, feat), BF16),
            vmem((group, feat), BF16),
            vmem((2, 2, side, feat), BF16),
            vmem((edges, feat), BF16),
            vmem((2 * side, feat), BF16),
            vmem((2 * feat, edges), BF16),
            vmem((edges, feat), BF16),
            vmem((edges, feat), F32),
            vmem((2 * cells, feat), F32),
            vmem((nodes, feat), F32),
            vmem((2, 2 * feat, feat), F32),
            vmem((2 * feat, feat), BF16),
            vmem((2 * feat, feat), BF16),
            vmem((nx, nz, piece, feat), BF16),
            vmem((nx - 1, nz, piece, feat), BF16),
            vmem((piece, feat), F32),
            vmem((nz - 1, piece, feat), BF16),
            vmem((nz - 1, piece, feat), BF16),
            vmem((NY, piece, feat), F32),
            vmem((nx, nz, piece, feat), BF16),
            vmem((2, nx, nz, piece, feat), BF16),
            vmem((8, L), F32),
            vmem((8, L), F32),
            vmem((nx, 8, L), F32),
            vmem((nz, 8, L), F32),
            vmem((NY, 8, L), F32),
            dma((12,)),
            dma((4, NY, 2)), dma((4, NY, 2)), dma((4, 3, 2)), dma((4, 3, 2)),
            dma((3, 7, 2)), dma((3, 7, 2)),
            dma((4,)), dma((4,)),
            dma((32,)), dma((32,)),
            dma((14,)), dma((14,)),
        ],
        compiler_params=pltpu.CompilerParams(
            collective_id=0, has_side_effects=True, vmem_limit_bytes=58 * 2**20),
    )(
        cluster_ids.reshape(nodes // L, L),
        halo_lists.reshape(2, side),
        edge_sources.reshape(group * K // L, L),
        b_edge_in.reshape(feat // L, L),
        node_feats, grad_out, w_edge_in, w_edge_out, w_unpool,
    )
    out = pl.pallas_call(
        store,
        out_shape=tuple(jax.ShapeDtypeStruct(shape, kind) for shape, kind in results),
        in_specs=[anywhere] * 5,
        out_specs=(anywhere,) * 5,
        scratch_shapes=[dma((5,))],
        compiler_params=pltpu.CompilerParams(vmem_limit_bytes=2**20),
    )(*[pltpu.with_memory_space_constraint(part, pltpu.VMEM) for part in parts])
    return out[0], out[1], out[2].reshape(feat), out[3], out[4]


def solution(mesh):
    return jax.shard_map(
        local,
        mesh=mesh,
        in_specs=(
            P(("coarse", "fine"), None), P(("coarse", "fine"), None), P(("coarse", "fine")),
            P("coarse"), P("coarse"), P(), P(), P(), P(),
        ),
        out_specs=(P(("coarse", "fine"), None), P(), P(), P(), P()),
        check_vma=False,
    )
```

time: 71.9 us -> 67.7 us (0.942)
  Pallas kernels: 70.9 us -> 66.8 us
    pallas_call x1, Pallas kernels: 69.5 us -> 65.4 us  [local(): pl.pallas_call(functools.partial(kernel, n_coarse, nx, edge_scale, cell_s...]
where the time goes in v3:
time: 67.7 us; the launch traced here: 67.6 us
  Pallas kernels  66.8 us (99%)
  between operations  0.8 us (1%)
    pallas_call x1, Pallas kernels, local(): pl.pallas_call(functools.partial(kernel, n_coarse, nx, edge_scale, cell_s...  65.4 us
    pallas_call x1, Pallas kernels, local(): pl.pallas_call(store, out_shape=tuple((jax.ShapeDtypeStruct(shape, kind)...  1.36 us

profile of v3, /device:TPU:1, one launch (start us, length us, event | category | flops | bytes accessed | tf_op | source)
XLA Modules:
  0.0 67.6 jit_solution(17940949855827124862)
XLA Ops:
  0.6 65.4 %shard_map.128 = (bf16[2048,256]{1,0:T(8,128)(2,1)S(1)}, f32[512,256]{1,0:T(8,128)S(1)}, f32[1,256]{1,0:T(1,128)S(1)}, f32[256,256]{1,0:T(8,128)S(1)}, f32[256,256]{1,0:T(8,128)S(1)}) custom-call(s32[16,128]{1,0:T(8,128)} %bitcast.6, s32[2,128]{1,0:T(2,128)} %bitcast.7, s32[64,128]{1,0:T(8,128)} %bitcast.5, bf16[2,128]{1,0:T(2,128)(2,1)} %bitcast.8, ...), custom_call_target="tpu_custom_call" | custom-call | tf_op jit(solution)/shard_map/pallas_call | solution.py:690
  66.0 1.4 %shard_map.129 = (bf16[2048,256]{1,0:T(8,128)(2,1)}, f32[512,256]{1,0:T(8,128)}, f32[1,256]{1,0:T(1,128)}, f32[256,256]{1,0:T(8,128)}, f32[256,256]{1,0:T(8,128)}) custom-call(bf16[2048,256]{1,0:T(8,128)(2,1)S(1)} %get-tuple-element.15.refs_0_, f32[512,256]{1,0:T(8,128)S(1)} %get-tuple-element.16.refs_1_, f32[1,256]{1,0:T(1,128)S(1)} %get-tuple-element.17.refs_2_, ...), custom_call_target="tpu_custom_call" | custom-call | tf_op jit(solution)/shard_map/pallas_call | solution.py:768

commit v4 on v3

--- a/solution.py
+++ b/solution.py
@@ -371,6 +371,11 @@
             send_sem=hs_s.at[2 + q], recv_sem=hs_r.at[2 + q],
             device_id={"coarse": to}, device_id_type=MESH)
 
+    outer = dot(src_mat_t[group:rows, :], gret[...])
+    hsend[1, 0] = outer[0:side].astype(BF16)
+    hsend[1, 1] = outer[side:2 * side].astype(BF16)
+    halo_back(0).start()
+    halo_back(1).start()
     w_part[0] = dot(turned[...], gret[...])
     gnew_t = jnp.concatenate([jnp.transpose(gnew)] * K, axis=1)
     w_part[1, 0:feat, :] = jnp.transpose(dot(gnew_t, hid[...]))
@@ -401,13 +406,6 @@
     near = sorted(range(nz), key=lambda d: (min(d, nz - d), d))
     lot = nz // 2
     pair_w.wait_recv()
-    for i in range(nx):
-        for p in range(nz):
-            at = pl.multiple_of((i * nz + lax.rem(z + far[p], nz)) * piece, piece)
-            w_rs[i, p] = (
-                w_part[core, pl.ds(at, piece), :] + w_pair_r[pl.ds(at, piece), :].astype(F32)
-            ).astype(BF16)
-
     def x_copy(d, h):
         part = pl.ds(h * lot, lot)
         return remote(w_rs.at[lax.rem(x + d, nx), part], w_x.at[d - 1, part],
@@ -426,13 +424,14 @@
         return remote(b_y.at[at], b_y.at[at], 10 + t, {"fine": place["step"][t]}, small)
 
     for h in range(2):
+        for i in range(nx):
+            for p in range(h * lot, (h + 1) * lot):
+                at = pl.multiple_of((i * nz + lax.rem(z + far[p], nz)) * piece, piece)
+                w_rs[i, p] = (
+                    w_part[core, pl.ds(at, piece), :] + w_pair_r[pl.ds(at, piece), :].astype(F32)
+                ).astype(BF16)
         for d in range(1, nx):
             x_copy(d, h).start()
-    outer = dot(src_mat_t[group:rows, :], gret[...])
-    hsend[1, 0] = outer[0:side].astype(BF16)
-    hsend[1, 1] = outer[side:2 * side].astype(BF16)
-    halo_back(0).start()
-    halo_back(1).start()
     pair_b.wait_recv()
     b_x[x] = b_pair_s[...] + b_pair_r[...]
     for d in range(1, nx):
@@ -518,13 +517,9 @@
     hb[pl.ds(pl.multiple_of(f * share, share), share), :] = returned.astype(BF16)
     ag2.start()
 
-    def take(y_at, first_pass):
-        at = pl.multiple_of(y_at * 2 * cells, 2 * cells)
-        part = dot(unpool_mat[:, pl.ds(at, 2 * cells)], gp[pl.ds(at, 2 * cells), :])
-        if first_pass:
-            acc[...] = part
-        else:
-            acc[...] += part
+    def take(y_at, core_at):
+        at = pl.multiple_of((y_at * 2 + core_at) * cells, cells)
+        return dot(unpool_mat[:, pl.ds(at, cells)], gp[pl.ds(at, cells), :])
 
     for t in (1, 2, 3):
         y_copy(t, y_of[NY - t]).wait_recv()
@@ -547,8 +542,9 @@
 
     for d in far[:-1]:
         z_back(d).start()
+    acc[...] = take(y, core)
     ag1.wait(0)
-    take(y, True)
+    acc[...] += take(y, 1 - core)
 
     def forward(h):
         for q in range(max(1, h * lot), (h + 1) * lot):
@@ -557,25 +553,29 @@
             x_back(d, h, x).start()
 
     forward(0)
-    for q in range(2):
-        for r in (1, 3, 2):
-            ag1.share(r, q)
     for r in (1, 3, 2):
+        ag1.share(r, 0)
+    forward(1)
+    for r in (1, 3):
+        ag1.share(r, 1)
+        acc[...] += take(y_of[NY - r], core)
         ag2.share(r)
-    forward(1)
+    ag1.share(2, 1)
+    ag2.share(2)
+    acc[...] += take(y_of[2], core)
     ag1.wait(4)
-    take(y_of[3], False)
+    acc[...] += take(y_of[3], 1 - core)
     ag1.wait(6)
-    take(y_of[1], False)
+    acc[...] += take(y_of[1], 1 - core)
     ag2.wait(0, 4, 6, 5)
     acc[...] += dot(list_mat[...], hb[...])
     ag1.wait(5)
-    at_far = pair_rows(2)
+    at_far = pl.multiple_of((y_of[2] * 2 + 1 - core) * cells, cells)
 
     @pl.loop(0, nodes // (2 * cells))
     def _(b):
         at = pl.ds(pl.multiple_of(b * 2 * cells, 2 * cells), 2 * cells)
-        part = dot(unpool_mat[at, pl.ds(at_far, 2 * cells)], gp[pl.ds(at_far, 2 * cells), :])
+        part = dot(unpool_mat[at, pl.ds(at_far, cells)], gp[pl.ds(at_far, cells), :])
         out_gf[at, :] = (go[at, :].astype(F32) + (acc[at, :] + part)).astype(BF16)
 
     for h in range(2):

time: 67.7 us -> 67 us (0.990)
  Pallas kernels: 66.8 us -> 66.1 us
where the time goes in v4:
time: 67 us; the launch traced here: 66.9 us
  Pallas kernels  66.1 us (99%)
  between operations  0.8 us (1%)
    pallas_call x1, Pallas kernels, local(): pl.pallas_call(functools.partial(kernel, n_coarse, nx, edge_scale, cell_s...  64.7 us
    pallas_call x1, Pallas kernels, local(): pl.pallas_call(store, out_shape=tuple((jax.ShapeDtypeStruct(shape, kind)...  1.36 us

profile of v4, /device:TPU:1, one launch (start us, length us, event | category | flops | bytes accessed | tf_op | source)
XLA Modules:
  0.0 66.9 jit_solution(17447128588667527611)
XLA Ops:
  0.6 64.7 %shard_map.128 = (bf16[2048,256]{1,0:T(8,128)(2,1)S(1)}, f32[512,256]{1,0:T(8,128)S(1)}, f32[1,256]{1,0:T(1,128)S(1)}, f32[256,256]{1,0:T(8,128)S(1)}, f32[256,256]{1,0:T(8,128)S(1)}) custom-call(s32[16,128]{1,0:T(8,128)} %bitcast.6, s32[2,128]{1,0:T(2,128)} %bitcast.7, s32[64,128]{1,0:T(8,128)} %bitcast.5, bf16[2,128]{1,0:T(2,128)(2,1)} %bitcast.8, ...), custom_call_target="tpu_custom_call" | custom-call | tf_op jit(solution)/shard_map/pallas_call | solution.py:690
  65.4 1.4 %shard_map.129 = (bf16[2048,256]{1,0:T(8,128)(2,1)}, f32[512,256]{1,0:T(8,128)}, f32[1,256]{1,0:T(1,128)}, f32[256,256]{1,0:T(8,128)}, f32[256,256]{1,0:T(8,128)}) custom-call(bf16[2048,256]{1,0:T(8,128)(2,1)S(1)} %get-tuple-element.15.refs_0_, f32[512,256]{1,0:T(8,128)S(1)} %get-tuple-element.16.refs_1_, f32[1,256]{1,0:T(1,128)S(1)} %get-tuple-element.17.refs_2_, ...), custom_call_target="tpu_custom_call" | custom-call | tf_op jit(solution)/shard_map/pallas_call | solution.py:768
